TPU v7x, 128 devices: a whole 4x4x4 slice. The times are simulated.
128 devices in a mesh: row: 16 (over y, z), col: 8 (over x, core).
Axes of the slice: x: 4, y: 4, z: 4, core: 2. Of those that a mesh axis runs over, the one named last changes fastest.
Arguments:
- grads: bfloat16 [128, 640, 5760], P(('row', 'col')), may hold values from -24 to 24
- residuals: bfloat16 [128, 640, 5760], P(('row', 'col')), may hold values from -4 to 4
- q_prev: float32 [5760, 8], replicated, may hold values from -6 to 6
- vec_grads: float32 [25600, 1280], P(('row', 'col')), may hold values from -24 to 24
Outputs:
- new_residuals: bfloat16 [128, 640, 5760], P(('row', 'col'))
- decompressed: float32 [640, 5760], P(('row', 'col'))
- q_next: float32 [5760, 8], replicated
- vec_mean: float32 [200, 1280], replicated
All inputs are finite; a program needn't handle non-finite values.
Results may differ from a plain program's by a relative error of at most 0.0077.
Values sent between devices are 32-bit elements; how exact they have to be, the bound alone decides.
No kernel may reach another device: no remote copies, remote signals or barrier semaphores. Data moves between devices by JAX's collectives and lax.ppermute only.
A program may use at most 64 MiB of HBM per device.

v0:
```python
import jax
import jax.numpy as jnp
from jax import lax
from jax.sharding import PartitionSpec as P


def on_device(grads, residuals, q_prev, vec_grads):
    replicas = lax.axis_size(("row", "col"))
    wide = grads[0].astype(jnp.float32) + residuals[0].astype(jnp.float32)
    compensated = wide.astype(jnp.bfloat16)
    p_part = jnp.dot(compensated, q_prev.astype(jnp.bfloat16), preferred_element_type=jnp.float32)
    p_total = lax.psum(p_part, ("row", "col"))
    gram = jnp.dot(p_total.T, p_total, precision=lax.Precision.HIGHEST)
    factor = jnp.linalg.cholesky(gram)
    p_orth = jax.scipy.linalg.solve_triangular(factor, p_total.T, lower=True).T
    p_half = p_orth.astype(jnp.bfloat16)
    q_local = lax.dot_general(
        compensated, p_half, (((0,), (0,)), ((), ())), preferred_element_type=jnp.float32
    )
    q_total = lax.psum(q_local, ("row", "col"))
    vec_total = lax.psum(vec_grads, ("row", "col"))
    fresh = wide - jnp.dot(p_orth, q_local.T, precision=lax.Precision.HIGHEST)
    new_residuals = fresh.astype(jnp.bfloat16)[None]
    own_rows = p_orth.shape[0] // replicas
    start = lax.axis_index(("row", "col")) * own_rows
    my_rows = lax.dynamic_slice_in_dim(p_orth, start, own_rows, 0)
    decompressed = jnp.dot(my_rows, q_total.T, precision=lax.Precision.HIGHEST) / replicas
    return (new_residuals, decompressed, q_total / replicas, vec_total / replicas)


def solution(mesh):
    return jax.shard_map(
        on_device,
        mesh=mesh,
        in_specs=(
            P(("row", "col"), None, None),
            P(("row", "col"), None, None),
            P(),
            P(("row", "col"), None),
        ),
        out_specs=(P(("row", "col"), None, None), P(("row", "col"), None), P(), P()),
        check_vma=False,
    )
```

profile of v0, /device:TPU:1, one launch (start us, length us, event | category | flops | bytes accessed | tf_op | source)
XLA Modules:
  0.0 273.8 jit_solution(70227065567688404)
XLA Ops:
  7.2 7.2 %fusion.3 = f32[640,8]{0,1:T(8,128)S(1)} fusion(bf16[1,640,5760]{2,1,0:T(8,128)(2,1)} %param.5, bf16[1,640,5760]{2,1,0:T(8,128)(2,1)} %param.4, f32[5760,8]{0,1:T(8,128)} %param.6), kind=kOutput, calls=%fused_computation.7 | convolution fusion | flops 73774080 | bytes 14950400 | tf_op jit(solution)/shard_map/dot_general | solution.py:11
  14.4 68.9 %psum.21 = f32[640,8]{0,1:T(8,128)S(1)} all-reduce(f32[640,8]{0,1:T(8,128)S(1)} %fusion.3), channel_id=1, replica_groups=mesh['row'=16,'col'=8] {'row','col'}, use_global_device_ids=true, to_apply=%region_0.0 | all-reduce | flops 5120 | bytes 40960 | tf_op jit(solution)/shard_map/psum | solution.py:12
  83.2 0.1 fusion.12
  83.4 0.1 copy.8
  83.5 0.7 cholesky.16
  84.2 0.1 select_reduce_fusion
  84.2 0.6 compare_reduce_fusion
  84.9 0.6 fusion.6
  85.5 0.6 custom-call.7
  86.2 0.2 fusion.7
  86.4 7.0 %fusion.2 = f32[5760,8]{0,1:T(8,128)S(1)} fusion(bf16[1,640,5760]{2,1,0:T(8,128)(2,1)} %param.5, bf16[1,640,5760]{2,1,0:T(8,128)(2,1)} %param.4, f32[8,640]{1,0:T(8,128)S(1)} %fusion.7), kind=kOutput, calls=%fused_computation.6 | convolution fusion | flops 73733120 | bytes 14950400 | tf_op jit(solution)/shard_map/dot_general | solution.py:17
  93.4 0.0 copy-start
  93.4 17.1 %fusion.1 = bf16[1,640,5760]{2,1,0:T(8,128)(2,1)} fusion(f32[8,640]{1,0:T(8,128)S(1)} %fusion.7, f32[5760,8]{0,1:T(8,128)S(1)} %fusion.2, bf16[1,640,5760]{2,1,0:T(8,128)(2,1)} %param.5, bf16[1,640,5760]{2,1,0:T(8,128)(2,1)} %param.4), kind=kOutput, calls=%fused_computation.4 | convolution fusion | flops 372326400 | bytes 22323200 | tf_op jit(solution)/shard_map/dot_general | solution.py:22
  110.5 0.0 copy-done
  110.5 0.0 all-reduce.3.cloned.1.call-start
  110.5 0.7 all-reduce.3.cloned.1.call-update
  111.2 149.8 %all-reduce.3.cloned.1.call-done = (f32[5760,8]{0,1:T(8,128)}, f32[200,1280]{1,0:T(8,128)}) async-done(((f32[5760,8]{0,1:T(8,128)}, f32[200,1280]{1,0:T(8,128)}), (f32[5760,8]{0,1:T(8,128)}, f32[200,1280]{1,0:T(8,128)})) %all-reduce.3.cloned.1.call-update) | async-done | bytes 1208336 | tf_op jit(solution)/shard_map/psum | solution.py:20
  261.0 1.6 broadcast_multiply_fusion.1
  262.6 2.0 convolution_multiply_fusion
  264.7 2.2 broadcast_multiply_fusion
  (1 shorter events, 0.0 us)
Async XLA Ops:
  93.4 17.1 %copy-start = (f32[5760,8]{0,1:T(8,128)}, f32[5760,8]{0,1:T(8,128)S(1)}, u32[]{:S(2)}) copy-start(f32[5760,8]{0,1:T(8,128)S(1)} %fusion.2) | copy-start | bytes 552964
  110.5 150.5 %all-reduce.3.cloned.1.call-start = ((), (), s32[]{:S(2)}) async-start(), calls=%async_computation | async-start | bytes 2416640 | tf_op jit(solution)/shard_map/psum | solution.py:20
Sparse Core Ops, SparseCore 0:
  116.9 144.1 all-reduce.2
where the time goes:
time: 274 us
  waiting for transfers between devices  150 us (55%)
  blocking collectives  68.9 us (25%)
  matrix products  33.7 us (12%)
  between operations  14.1 us (5%)
  other arithmetic  6.56 us (2%)
    psum x1, waiting for transfers between devices, on_device(): q_total = lax.psum(q_local, ('row', 'col'))  150 us
    psum x1, blocking collectives, on_device(): p_total = lax.psum(p_part, ('row', 'col'))  68.9 us
    dot_general x1, matrix products, on_device(): fresh = wide - jnp.dot(p_orth, q_local.T, precision=lax.Precision.HIGHEST)  17.1 us
    dot_general x1, matrix products, on_device(): jnp.dot(compensated, q_prev.astype(jnp.bfloat16), preferred_element_type=...  7.21 us
    dot_general x1, matrix products, on_device(): lax.dot_general(compensated, p_half, (((0,), (0,)), ((), ())), preferred_...  6.98 us
  transfers between devices with their start and end apart: 1, of which 1 were waited for; matrix products, arithmetic and copies ran while one was open for 0% of the time, Pallas kernels for 0%

commit v1 on v0

v1 whole, which is shorter than its diff:
```python
import jax
import jax.numpy as jnp
from jax import lax
from jax.experimental import pallas as pl
from jax.experimental.pallas import tpu as pltpu
from jax.sharding import PartitionSpec as P

AXES = ("row", "col")
MIB = 1 << 20
LANES = 128
SUBS = 8
F32 = jnp.float32
BF16 = jnp.bfloat16
RING_BIT = {"x": 1, "z": 3, "y": 5}
AROUND = ("x", "y")
P_HOPS = (("x0", "x1", "y0", "z0", "z1", "y1"),) * 2
V_HOPS = (("y0", "z0", "x0", "x1", "z1", "y1"), ("z0", "x0", "y0", "y1", "x1", "z1"))
Q_HOPS = (("x0", "y0", "x1", "z0", "y1", "z1"), ("x1", "y1", "x0", "z1", "y0", "z0"))
HALVINGS = 2


def partner(index, hops):
    ring, level = hops[index & 1]
    bit = RING_BIT[ring]
    if level == "0":
        return index ^ (1 << bit)
    return index ^ ((3 if ring in AROUND else 2) << bit)


def swap(x, hops, step):
    pair = (hops[0][step], hops[1][step])
    return lax.ppermute(x, AXES, [(i, partner(i, pair)) for i in range(lax.axis_size(AXES))])


def swap_cores(x):
    return lax.ppermute(x, AXES, [(i, i ^ 1) for i in range(lax.axis_size(AXES))])


def place():
    return lax.axis_index("row") * lax.axis_size("col") + lax.axis_index("col")


def keeps_high(index, step):
    def of(hop):
        bit = RING_BIT[hop[0]]
        low, high = (index >> bit) & 1, (index >> (bit + 1)) & 1
        return low ^ high if hop[0] in AROUND else low

    core = index & 1
    return jnp.where(core == 0, of(V_HOPS[0][step]), of(V_HOPS[1][step])) == 1


def in_hbm(x):
    return pltpu.with_memory_space_constraint(x, pltpu.HBM)


def blocks(count):
    return jax.ShapeDtypeStruct((count, SUBS, LANES), F32)


def call(body, operands, outs, after=(), limit=12, **options):
    count = len(operands)

    def kernel(*refs):
        body(*refs[:count], *refs[count + len(after) :])

    return pl.pallas_call(
        kernel,
        in_specs=[pl.BlockSpec(memory_space=pltpu.VMEM)] * count + [pl.BlockSpec(memory_space=pl.ANY)] * len(after),
        out_specs=jax.tree.map(lambda _: pl.BlockSpec(memory_space=pltpu.VMEM), outs),
        out_shape=outs,
        compiler_params=pltpu.CompilerParams(vmem_limit_bytes=limit * MIB),
        **options,
    )(*operands, *after)


def left_product(grads, residuals, q_rows):
    _, rows, cols = grads.shape
    rank = q_rows.shape[0]
    parts = rows // LANES

    def body(g_hbm, r_hbm, q_hbm, p_ref, c_ref, g_ref, r_ref, q_ref, sems):
        copies = [pltpu.make_async_copy(q_hbm, q_ref, sems.at[2 * parts])]
        for i in range(parts):
            own = pl.ds(i * LANES, LANES)
            copies.append(pltpu.make_async_copy(g_hbm.at[0, own], g_ref.at[own], sems.at[2 * i]))
            copies.append(pltpu.make_async_copy(r_hbm.at[0, own], r_ref.at[own], sems.at[2 * i + 1]))
        for copy in copies:
            copy.start()
        copies[0].wait()
        q_half = q_ref[...].astype(BF16)
        for i in range(parts):
            own = slice(i * LANES, (i + 1) * LANES)
            copies[2 * i + 1].wait()
            copies[2 * i + 2].wait()
            compensated = (g_ref[own, :].astype(F32) + r_ref[own, :].astype(F32)).astype(BF16)
            c_ref[own, :] = compensated
            p_ref[i] = lax.dot_general(
                q_half, compensated, (((1,), (1,)), ((), ())), preferred_element_type=F32
            )

    whole = pltpu.VMEM((rows, cols), BF16)
    return pl.pallas_call(
        body,
        in_specs=[pl.BlockSpec(memory_space=pltpu.HBM)] * 3,
        out_specs=[pl.BlockSpec(memory_space=pltpu.VMEM)] * 4,
        out_shape=[blocks(parts), whole, whole, whole],
        scratch_shapes=[pltpu.VMEM((rank, cols), F32), pltpu.SemaphoreType.DMA((2 * parts + 1,))],
        compiler_params=pltpu.CompilerParams(vmem_limit_bytes=32 * MIB),
    )(in_hbm(grads), in_hbm(residuals), in_hbm(q_rows))


def right_product(p_tiles, p_other, compensated, after):
    tiles, rank, _ = p_tiles.shape
    rows, cols = compensated.shape
    out_tiles = cols // LANES
    count = (out_tiles + 1) // 2

    def body(p_ref, o_ref, c_ref, orth_ref, q_ref, keep_ref, send_ref):
        total = jnp.concatenate([p_ref[t] + o_ref[t] for t in range(tiles)], axis=1)
        gram = lax.dot_general(
            total, total, (((1,), (1,)), ((), ())), precision=lax.Precision.HIGHEST, preferred_element_type=F32
        )
        sub = lax.broadcasted_iota(jnp.int32, (rank, 1), 0)
        for j in range(rank):
            scale = lax.rsqrt(gram[j : j + 1, j : j + 1])
            column = jnp.where(sub > j, gram[:, j : j + 1] * scale, 0.0)
            gram_row, total_row = gram[j : j + 1, :] * scale, total[j : j + 1, :] * scale
            gram = jnp.where(sub == j, gram_row, gram - column * gram_row)
            total = jnp.where(sub == j, total_row, total - column * total_row)
        orth_ref[...] = total
        half = total.astype(BF16)
        step = 9 * LANES
        for s in range(0, cols, step):
            part = lax.dot_general(
                half, c_ref[:, s : s + step], (((1,), (0,)), ((), ())), preferred_element_type=F32
            )
            for t in range(step // LANES):
                q_ref[s // LANES + t] = part[:, t * LANES : (t + 1) * LANES]
        core = place() & 1

        @pl.when(core == 0)
        def _():
            keep_ref[...] = q_ref[:count]
            send_ref[...] = q_ref[out_tiles - count :]

        @pl.when(core == 1)
        def _():
            send_ref[...] = q_ref[:count]
            keep_ref[...] = q_ref[out_tiles - count :]

    outs = [jax.ShapeDtypeStruct((rank, rows), F32), blocks(out_tiles), blocks(count), blocks(count)]
    return call(body, [p_tiles, p_other, compensated], outs, after)


def thirds(x):
    a = x.astype(BF16)
    rest = x - a.astype(F32)
    b = rest.astype(BF16)
    return a, b, (rest - b.astype(F32)).astype(BF16)


def factors(orth, q_tiles, own_rows, after):
    rank, rows = orth.shape
    tiles = q_tiles.shape[0]

    def body(p_ref, q_ref, left_ref, right_ref, own_ref):
        a, b, c = thirds(p_ref[...])
        left_ref[...] = jnp.concatenate([a, a, b, a, b, c], axis=0)
        for t in range(tiles):
            a, b, c = thirds(q_ref[t])
            right_ref[:, t * LANES : (t + 1) * LANES] = jnp.concatenate([a, b, a, c, b, a], axis=0)
        column = lax.broadcasted_iota(jnp.int32, (SUBS, rows), 1)
        row = lax.broadcasted_iota(jnp.int32, (SUBS, rows), 0)
        chosen = jnp.where(column == place() * own_rows + row, 1.0, 0.0)
        own_ref[...] = lax.dot_general(
            chosen, p_ref[...], (((1,), (1,)), ((), ())), precision=lax.Precision.HIGHEST, preferred_element_type=F32
        )

    outs = [
        jax.ShapeDtypeStruct((6 * rank, rows), BF16),
        jax.ShapeDtypeStruct((6 * rank, tiles * LANES), BF16),
        jax.ShapeDtypeStruct((SUBS, rank), F32),
    ]
    return call(body, [orth, q_tiles], outs, after)


def residual_rows(piece, left, right, grads, residuals, before, after):
    rows, cols = grads.shape
    step = 9 * LANES
    parts = cols // step
    own = slice(piece * LANES, (piece + 1) * LANES)

    def body(l_ref, r_ref, g_ref, e_ref, *rest):
        out_hbm, done_ref, stage, sems = rest[-4:]
        copies = []
        for j in range(parts):
            here = slice(j * step, (j + 1) * step)
            wide = g_ref[own, here].astype(F32) + e_ref[own, here].astype(F32)
            away = lax.dot_general(
                l_ref[:, own], r_ref[:, here], (((0,), (0,)), ((), ())), preferred_element_type=F32
            )
            stage[:, here] = (wide - away).astype(BF16)
            copies.append(
                pltpu.make_async_copy(stage.at[:, here], out_hbm.at[0, own, here], sems.at[j])
            )
            copies[-1].start()
        done_ref[...] = jnp.zeros_like(done_ref)
        for copy in copies:
            copy.wait()

    operands = [left, right, grads, residuals]
    vmem, anywhere = pl.BlockSpec(memory_space=pltpu.VMEM), pl.BlockSpec(memory_space=pl.ANY)
    others = ([] if before is None else [before]) + list(after)
    return pl.pallas_call(
        body,
        in_specs=[vmem] * 4 + [anywhere] * len(others),
        out_specs=[pl.BlockSpec(memory_space=pltpu.HBM), vmem],
        out_shape=[jax.ShapeDtypeStruct((1, rows, cols), BF16), blocks(1)],
        scratch_shapes=[pltpu.VMEM((LANES, cols), BF16), pltpu.SemaphoreType.DMA((parts,))],
        input_output_aliases={} if before is None else {4: 0},
        compiler_params=pltpu.CompilerParams(vmem_limit_bytes=12 * MIB),
    )(*operands, *others)


def add(a, b, after=()):
    def body(a_ref, b_ref, out_ref):
        out_ref[...] = a_ref[...] + b_ref[...]

    return call(body, [a, b], blocks(a.shape[0]), after)


def split_vectors(vec, after):
    height, width = vec.shape
    across = width // LANES
    half = height // SUBS * across // 2

    def body(vec_ref, keep_ref, send_ref):
        def copy(low_ref, high_ref):
            for t in range(2 * half):
                y, x = t // across * SUBS, t % across * LANES
                tile = vec_ref[y : y + SUBS, x : x + LANES]
                if t < half:
                    low_ref[t] = tile
                else:
                    high_ref[t - half] = tile

        core = place() & 1

        @pl.when(core == 0)
        def _():
            copy(keep_ref, send_ref)

        @pl.when(core == 1)
        def _():
            copy(send_ref, keep_ref)

    return call(body, [vec], [blocks(half), blocks(half)], after)


def halve(step, a, b, after):
    size = a.shape[0]
    part = (size + 1) // 2

    def body(a_ref, b_ref, keep_ref, send_ref):
        low = a_ref[:part] + b_ref[:part]
        high = a_ref[size - part :] + b_ref[size - part :]
        flag = keeps_high(place(), step)
        keep_ref[...] = jnp.where(flag, high, low)
        send_ref[...] = jnp.where(flag, low, high)

    return call(body, [a, b], [blocks(part), blocks(part)], after)


def join(step, size, mine, other, after):
    part = mine.shape[0]

    def body(mine_ref, other_ref, out_ref):
        flag = keeps_high(place(), step)
        mine, other = mine_ref[...], other_ref[...]
        out_ref[size - part :] = jnp.where(flag, mine, other)
        out_ref[:part] = jnp.where(flag, other, mine)

    return call(body, [mine, other], blocks(size), after)


def join_vectors(mine, other, shape, replicas, after):
    height, width = shape
    across = width // LANES
    half = mine.shape[0]

    def body(mine_ref, other_ref, vec_ref):
        def copy(low_ref, high_ref):
            for t in range(2 * half):
                y, x = t // across * SUBS, t % across * LANES
                tile = low_ref[t] if t < half else high_ref[t - half]
                vec_ref[y : y + SUBS, x : x + LANES] = tile * (1.0 / replicas)

        core = place() & 1

        @pl.when(core == 0)
        def _():
            copy(mine_ref, other_ref)

        @pl.when(core == 1)
        def _():
            copy(other_ref, mine_ref)

    return call(body, [mine, other], jax.ShapeDtypeStruct(shape, F32), after)


def finish(mine, other, own, own_rows, tiles, replicas):
    count, rank, _ = mine.shape

    def body(mine_ref, other_ref, own_ref, q_ref, d_ref):
        def write(low_ref, high_ref):
            columns = [own_ref[:own_rows, k : k + 1] for k in range(rank)]
            for t in range(tiles):
                mean = (low_ref[t] if t < count else high_ref[t - tiles + count]) * (1.0 / replicas)
                q_ref[:, t * LANES : (t + 1) * LANES] = mean
                out = columns[0] * mean[0:1, :]
                for k in range(1, rank):
                    out = out + columns[k] * mean[k : k + 1, :]
                d_ref[:, t * LANES : (t + 1) * LANES] = out

        core = place() & 1

        @pl.when(core == 0)
        def _():
            write(mine_ref, other_ref)

        @pl.when(core == 1)
        def _():
            write(other_ref, mine_ref)

    outs = [
        jax.ShapeDtypeStruct((rank, tiles * LANES), F32),
        jax.ShapeDtypeStruct((own_rows, tiles * LANES), F32),
    ]
    return call(body, [mine, other, own], outs)


def on_device(grads, residuals, q_prev, vec_grads):
    devices = lax.axis_size(AXES)
    steps = len(P_HOPS[0])
    p_tiles, compensated, g_here, r_here = left_product(grads, residuals, q_prev.T)

    got = swap(p_tiles, P_HOPS, 0)
    v_keep, v_send = split_vectors(vec_grads, [p_tiles])
    half = v_keep.shape[0]
    v_got = swap_cores(v_send)
    p_tiles = add(p_tiles, got, [v_send])
    sizes = [half]
    v_step = 0

    def advance(after):
        nonlocal v_keep, v_send, v_got, v_step
        if v_step < HALVINGS:
            v_keep, v_send = halve(v_step, v_keep, v_got, after)
            sizes.append(v_keep.shape[0])
            v_got = swap(v_send, V_HOPS, v_step)
        elif v_step < steps:
            v_keep = v_send = add(v_keep, v_got, after)
            v_got = swap(v_send, V_HOPS, v_step)
        elif v_step < steps + HALVINGS:
            back = steps + HALVINGS - 1 - v_step
            if back == HALVINGS - 1:
                v_keep = add(v_keep, v_got, after)
            else:
                v_keep = join(back + 1, sizes[back + 1], v_keep, v_got, after)
            v_send = v_keep
            v_got = swap(v_send, V_HOPS, back)
        elif v_step == steps + HALVINGS:
            v_send = v_keep = join(0, half, v_keep, v_got, after)
            v_got = swap_cores(v_send)
        elif v_step == steps + HALVINGS + 1:
            v_send = v_keep = join_vectors(v_keep, v_got, vec_grads.shape, devices, after)
        v_step += 1

    for step in range(1, steps):
        got = swap(p_tiles, P_HOPS, step)
        advance([p_tiles])
        p_tiles = add(p_tiles, got, [v_send])

    orth, q_tiles, q_keep, q_send = right_product(p_tiles, swap_cores(p_tiles), compensated, [])
    got = swap_cores(q_send)
    left, right, own = factors(orth, q_tiles, orth.shape[1] // devices, [q_send])
    q_sum = add(q_keep, got, [own])
    fresh = None
    pieces = grads.shape[1] // LANES
    for step in range(steps):
        got = swap(q_sum, Q_HOPS, step)
        advance([q_sum])
        after = [v_send]
        piece = step - (steps - pieces)
        if piece >= 0:
            fresh, done = residual_rows(piece, left, right, g_here, r_here, fresh, [q_sum, v_send])
            after = [done]
        q_sum = add(q_sum, got, after)

    other = swap_cores(q_sum)
    q_next, decompressed = finish(q_sum, other, own, orth.shape[1] // devices, q_tiles.shape[0], devices)
    return (fresh, decompressed, q_next.T, v_keep)


def solution(mesh):
    return jax.shard_map(
        on_device,
        mesh=mesh,
        in_specs=(P(AXES, None, None), P(AXES, None, None), P(), P(AXES, None)),
        out_specs=(P(AXES, None, None), P(AXES, None), P(), P()),
        check_vma=False,
    )
```

time: 274 us -> 88.2 us (0.32)
  waiting for transfers between devices: 150 us -> 19 us
  blocking collectives: 68.9 us -> 0 us
  starting transfers between devices: 0.01 us -> 48.4 us
  matrix products: 33.7 us -> 0 us
  Pallas kernels: 0 us -> 18.5 us
  between operations: 14.1 us -> 0.84 us
  other arithmetic: 6.56 us -> 0 us
    psum x1 -> x0, waiting for transfers between devices: 150 us -> none  [on_device(): q_total = lax.psum(q_local, ('row', 'col'))]
    psum x1 -> x0, blocking collectives: 68.9 us -> none  [on_device(): p_total = lax.psum(p_part, ('row', 'col'))]
    ppermute x0 -> x25, starting transfers between devices: none -> 48.4 us  [the longest x20 32.2 us: swap(): lax.ppermute(x, AXES, [(i, partner(i, pair)) for i in range(lax.axis_size...]
    dot_general x5 -> x0, matrix products: 33.5 us -> none  [the longest x1 17.1 us: on_device(): fresh = wide - jnp.dot(p_orth, q_local.T, precision=lax.Precision.HIGHEST)]
    ppermute x0 -> x25, waiting for transfers between devices: none -> 19 us  [the longest x20 16.5 us: swap(): lax.ppermute(x, AXES, [(i, partner(i, pair)) for i in range(lax.axis_size...]
    pallas_call x0 -> x33, Pallas kernels: none -> 18.5 us  [the longest x5 7.23 us: residual_rows(): pl.pallas_call(body, in_specs=[vmem] * 4 + [anywhere] * len(others), out_...]
    div x3 -> x0, other arithmetic: 3.86 us -> none  [the longest x1 2.24 us: on_device(): vec_total / replicas]
  transfers between devices with their start and end apart: 1 -> 25, of which waited for: 1 -> 17; matrix products, arithmetic and copies ran while one was open for 0% -> 0% of each run, Pallas kernels for 0% -> 12%
where the time goes in v1:
time: 88.2 us; the launch traced here: 88 us
  starting transfers between devices  48.4 us (55%)
  waiting for transfers between devices  19 us (22%)
  Pallas kernels  18.5 us (21%)
  local copies, waits for them, and re-layouts  1.22 us (1%)
    ppermute x20, starting transfers between devices, swap(): lax.ppermute(x, AXES, [(i, partner(i, pair)) for i in range(lax.axis_size...  32.2 us
    ppermute x20, waiting for transfers between devices, swap(): lax.ppermute(x, AXES, [(i, partner(i, pair)) for i in range(lax.axis_size...  16.5 us
    ppermute x5, starting transfers between devices, swap_cores(): lax.ppermute(x, AXES, [(i, i ^ 1) for i in range(lax.axis_size(AXES))])  16.2 us
    pallas_call x5, Pallas kernels, residual_rows(): pl.pallas_call(body, in_specs=[vmem] * 4 + [anywhere] * len(others), out_...  7.23 us
    pallas_call x1, Pallas kernels, left_product(): pl.pallas_call(body, in_specs=[pl.BlockSpec(memory_space=pltpu.HBM)] * 3,...  6.61 us
    pallas_call x27, Pallas kernels, call(): pl.pallas_call(kernel, in_specs=[pl.BlockSpec(memory_space=pltpu.VMEM)] *...  4.67 us
    ppermute x5, waiting for transfers between devices, swap_cores(): lax.ppermute(x, AXES, [(i, i ^ 1) for i in range(lax.axis_size(AXES))])  2.51 us
  transfers between devices with their start and end apart: 25, of which 17 were waited for; matrix products, arithmetic and copies ran while one was open for 0% of the time, Pallas kernels for 12%

profile of v1, /device:TPU:1, one launch (start us, length us, event | category | flops | bytes accessed | tf_op | source)
XLA Modules:
  0.0 88.0 jit_solution(14986464211496513785)
XLA Ops:
  0.6 6.6 %shard_map.75 = (f32[5,8,128]{2,1,0:T(8,128)S(1)}, bf16[640,5760]{1,0:T(8,128)(2,1)S(1)}, bf16[640,5760]{1,0:T(8,128)(2,1)S(1)}, bf16[640,5760]{1,0:T(8,128)(2,1)S(1)}) custom-call(bf16[1,640,5760]{2,1,0:T(8,128)(2,1)} %g_hbm.1, bf16[1,640,5760]{2,1,0:T(8,128)(2,1)} %r_hbm.1, f32[8,5760]{1,0:T(8,128)} %bitcast.2), custom_call_target="tpu_custom_call" | custom-call | tf_op jit(solution)/shard_map/pallas_call | solution.py:103
  7.4 1.5 %collective-permute-start.2 = (f32[125,8,128]{2,1,0:T(8,128)S(1)}, f32[125,8,128]{2,1,0:T(8,128)S(1)}, u32[]{:S(2)}, u32[]{:S(2)}) collective-permute-start(f32[125,8,128]{2,1,0:T(8,128)S(1)} %get-tuple-element.34.refs_2_), channel_id=1, source_target_pairs={{0,1},{1,0},{2,3},{3,2},{4,5},{5,4},{6,7},{7,6},{8,9},{9,8},{10,11... | collective-permute-start | bytes 1536008 | tf_op jit(solution)/shard_map/ppermute | solution.py:36
  11.6 1.8 %collective-permute-start.4 = (f32[63,8,128]{2,1,0:T(8,128)S(1)}, f32[63,8,128]{2,1,0:T(8,128)S(1)}, u32[]{:S(2)}, u32[]{:S(2)}) collective-permute-start(f32[63,8,128]{2,1,0:T(8,128)S(1)} %get-tuple-element.36.refs_2_), channel_id=1, source_target_pairs={{0,32},{1,9},{2,34},{3,11},{4,36},{5,13},{6,38},{7,15},{8,40},{9,1... | collective-permute-start | bytes 774152 | tf_op jit(solution)/shard_map/ppermute | solution.py:32
  13.4 2.5 %collective-permute-start.1 = (f32[5,8,128]{2,1,0:T(8,128)S(1)}, f32[5,8,128]{2,1,0:T(8,128)S(1)}, u32[]{:S(2)}, u32[]{:S(2)}) collective-permute-start(f32[5,8,128]{2,1,0:T(8,128)S(1)} %shard_map.77.refs_2_.refs_0_), channel_id=1, source_target_pairs={{0,6},{1,7},{2,4},{3,5},{4,2},{5,3},{6,0},{7,1},{8,14},{9,15},{10,... | collective-permute-start | bytes 61448 | tf_op jit(solution)/shard_map/ppermute | solution.py:32
  21.4 1.4 %collective-permute-start.8 = (f32[32,8,128]{2,1,0:T(8,128)S(1)}, f32[32,8,128]{2,1,0:T(8,128)S(1)}, u32[]{:S(2)}, u32[]{:S(2)}) collective-permute-start(f32[32,8,128]{2,1,0:T(8,128)S(1)} %shard_map.82.refs_2_.refs_0_), channel_id=1, source_target_pairs={{0,2},{1,33},{2,0},{3,35},{4,6},{5,37},{6,4},{7,39},{8,10},{9,41},... | collective-permute-start | bytes 393224 | tf_op jit(solution)/shard_map/ppermute | solution.py:32
  22.8 1.5 %collective-permute-start.5 = (f32[5,8,128]{2,1,0:T(8,128)S(1)}, f32[5,8,128]{2,1,0:T(8,128)S(1)}, u32[]{:S(2)}, u32[]{:S(2)}) collective-permute-start(f32[5,8,128]{2,1,0:T(8,128)S(1)} %shard_map.81.refs_2_.refs_0_), channel_id=1, source_target_pairs={{0,8},{1,9},{2,10},{3,11},{4,12},{5,13},{6,14},{7,15},{8,0},{9,1},... | collective-permute-start | bytes 61448 | tf_op jit(solution)/shard_map/ppermute | solution.py:32
  25.5 2.8 %collective-permute-start.10 = (f32[32,8,128]{2,1,0:T(8,128)S(1)}, f32[32,8,128]{2,1,0:T(8,128)S(1)}, u32[]{:S(2)}, u32[]{:S(2)}) collective-permute-start(f32[32,8,128]{2,1,0:T(8,128)S(1)} %shard_map.84.refs_2_.refs_0_), channel_id=1, source_target_pairs={{0,6},{1,97},{2,4},{3,99},{4,2},{5,101},{6,0},{7,103},{8,14},{9,10... | collective-permute-start | bytes 393224 | tf_op jit(solution)/shard_map/ppermute | solution.py:32
  28.4 3.4 %collective-permute-start.7 = (f32[5,8,128]{2,1,0:T(8,128)S(1)}, f32[5,8,128]{2,1,0:T(8,128)S(1)}, u32[]{:S(2)}, u32[]{:S(2)}) collective-permute-start(f32[5,8,128]{2,1,0:T(8,128)S(1)} %shard_map.83.refs_2_.refs_0_), channel_id=1, source_target_pairs={{0,16},{1,17},{2,18},{3,19},{4,20},{5,21},{6,22},{7,23},{8,24},{9,... | collective-permute-start | bytes 61448 | tf_op jit(solution)/shard_map/ppermute | solution.py:32
  33.1 2.5 %collective-permute-start.14 = (f32[32,8,128]{2,1,0:T(8,128)S(1)}, f32[32,8,128]{2,1,0:T(8,128)S(1)}, u32[]{:S(2)}, u32[]{:S(2)}) collective-permute-start(f32[32,8,128]{2,1,0:T(8,128)S(1)} %shard_map.86.refs_2_.refs_0_), channel_id=1, source_target_pairs={{0,16},{1,7},{2,18},{3,5},{4,20},{5,3},{6,22},{7,1},{8,24},{9,15},... | collective-permute-start | bytes 393224 | tf_op jit(solution)/shard_map/ppermute | solution.py:32
  36.8 8.6 %collective-permute-start.11 = (f32[5,8,128]{2,1,0:T(8,128)S(1)}, f32[5,8,128]{2,1,0:T(8,128)S(1)}, u32[]{:S(2)}, u32[]{:S(2)}) collective-permute-start(f32[5,8,128]{2,1,0:T(8,128)S(1)} %shard_map.87.refs_0_), channel_id=1, source_target_pairs={{0,1},{1,0},{2,3},{3,2},{4,5},{5,4},{6,7},{7,6},{8,9},{9,8},{10,11... | collective-permute-start | bytes 61448 | tf_op jit(solution)/shard_map/ppermute | solution.py:36
  46.2 1.9 %shard_map.88 = (f32[8,640]{1,0:T(8,128)S(1)}, f32[45,8,128]{2,1,0:T(8,128)S(1)}, f32[23,8,128]{2,1,0:T(8,128)S(1)}, f32[23,8,128]{2,1,0:T(8,128)S(1)}) custom-call(f32[5,8,128]{2,1,0:T(8,128)S(1)} %shard_map.87.refs_0_, f32[5,8,128]{2,1,0:T(8,128)S(1)} %collective-permute-done.11.refs_1_, bf16[640,5760]{1,0:T(8,128)(2,1)S(1)} %get-tuple-element.40.refs_2_), custom_call_target="tpu_custom_call" | custom-call | tf_op jit(solution)/shard_map/pallas_call | solution.py:67
  49.6 1.8 %collective-permute-start.15 = (f32[32,8,128]{2,1,0:T(8,128)S(1)}, f32[32,8,128]{2,1,0:T(8,128)S(1)}, u32[]{:S(2)}, u32[]{:S(2)}) collective-permute-start(f32[32,8,128]{2,1,0:T(8,128)S(1)} %shard_map.91.refs_2_.refs_0_), channel_id=1, source_target_pairs={{0,96},{1,17},{2,98},{3,19},{4,100},{5,21},{6,102},{7,23},{8,104},... | collective-permute-start | bytes 393224 | tf_op jit(solution)/shard_map/ppermute | solution.py:32
  51.7 4.3 %collective-permute-done.13.refs_1_ = f32[23,8,128]{2,1,0:T(8,128)S(1)} collective-permute-done((f32[23,8,128]{2,1,0:T(8,128)S(1)}, f32[23,8,128]{2,1,0:T(8,128)S(1)}, u32[]{:S(2)}, u32[]{:S(2)}) %collective-permute-start.13) | collective-permute-done | bytes 94240 | tf_op jit(solution)/shard_map/ppermute | solution.py:32
  56.1 2.6 %collective-permute-start.16 = (f32[23,8,128]{2,1,0:T(8,128)S(1)}, f32[23,8,128]{2,1,0:T(8,128)S(1)}, u32[]{:S(2)}, u32[]{:S(2)}) collective-permute-start(f32[23,8,128]{2,1,0:T(8,128)S(1)} %shard_map.92.refs_2_.rest_0_.refs_0_), channel_id=1, source_target_pairs={{0,32},{1,97},{2,34},{3,99},{4,36},{5,101},{6,38},{7,103},{8,40},{... | collective-permute-start | bytes 282632 | tf_op jit(solution)/shard_map/ppermute | solution.py:32
  58.7 1.4 %shard_map.94 = (bf16[1,640,5760]{2,1,0:T(8,128)(2,1)}, f32[1,8,128]{2,1,0:T(8,128)S(1)}) custom-call(bf16[48,640]{1,0:T(8,128)(2,1)S(1)} %get-tuple-element.44.l_ref, bf16[48,5760]{1,0:T(8,128)(2,1)S(1)} %get-tuple-element.45.r_ref, bf16[640,5760]{1,0:T(8,128)(2,1)S(1)} %get-tuple-element.46.g_ref, bf16[640,5760]{1,0:T(8,128)(2,1)S(1)} %get-tuple-element.47.e_ref, ...), custom_call_target="tpu_custom_call" | custom-call | tf_op jit(solution)/shard_map/pallas_call | solution.py:215
  61.1 1.4 %collective-permute-start.18 = (f32[23,8,128]{2,1,0:T(8,128)S(1)}, f32[23,8,128]{2,1,0:T(8,128)S(1)}, u32[]{:S(2)}, u32[]{:S(2)}) collective-permute-start(f32[23,8,128]{2,1,0:T(8,128)S(1)} %shard_map.95.refs_2_.rest_1_.refs_0_), channel_id=1, source_target_pairs={{0,6},{1,3},{2,4},{3,1},{4,2},{5,7},{6,0},{7,5},{8,14},{9,11},{10,... | collective-permute-start | bytes 282632 | tf_op jit(solution)/shard_map/ppermute | solution.py:32
  62.5 1.5 %shard_map.97 = (bf16[1,640,5760]{2,1,0:T(8,128)(2,1)}, f32[1,8,128]{2,1,0:T(8,128)S(1)}) custom-call(bf16[48,640]{1,0:T(8,128)(2,1)S(1)} %get-tuple-element.44.l_ref, bf16[48,5760]{1,0:T(8,128)(2,1)S(1)} %get-tuple-element.45.r_ref, bf16[640,5760]{1,0:T(8,128)(2,1)S(1)} %get-tuple-element.46.g_ref, ...), custom_call_target="tpu_custom_call", output_to_operand_aliasing={{0}: (4, {})} | custom-call | tf_op jit(solution)/shard_map/pallas_call | solution.py:215
  64.8 1.6 %collective-permute-done.19.refs_1_ = f32[63,8,128]{2,1,0:T(8,128)S(1)} collective-permute-done((f32[63,8,128]{2,1,0:T(8,128)S(1)}, f32[63,8,128]{2,1,0:T(8,128)S(1)}, u32[]{:S(2)}, u32[]{:S(2)}) %collective-permute-start.19) | collective-permute-done | bytes 258080 | tf_op jit(solution)/shard_map/ppermute | solution.py:32
  66.5 1.7 %collective-permute-start.21 = (f32[125,8,128]{2,1,0:T(8,128)S(1)}, f32[125,8,128]{2,1,0:T(8,128)S(1)}, u32[]{:S(2)}, u32[]{:S(2)}) collective-permute-start(f32[125,8,128]{2,1,0:T(8,128)S(1)} %shard_map.99.rest_2_.refs_0_), channel_id=1, source_target_pairs={{0,1},{1,0},{2,3},{3,2},{4,5},{5,4},{6,7},{7,6},{8,9},{9,8},{10,11... | collective-permute-start | bytes 1536008 | tf_op jit(solution)/shard_map/ppermute | solution.py:36
  68.2 3.3 %collective-permute-start.20 = (f32[23,8,128]{2,1,0:T(8,128)S(1)}, f32[23,8,128]{2,1,0:T(8,128)S(1)}, u32[]{:S(2)}, u32[]{:S(2)}) collective-permute-start(f32[23,8,128]{2,1,0:T(8,128)S(1)} %shard_map.98.refs_2_.rest_1_.refs_0_), channel_id=1, source_target_pairs={{0,8},{1,17},{2,10},{3,19},{4,12},{5,21},{6,14},{7,23},{8,0},{9,25... | collective-permute-start | bytes 282632 | tf_op jit(solution)/shard_map/ppermute | solution.py:32
  71.5 1.5 %shard_map.100 = (bf16[1,640,5760]{2,1,0:T(8,128)(2,1)}, f32[1,8,128]{2,1,0:T(8,128)S(1)}) custom-call(bf16[48,640]{1,0:T(8,128)(2,1)S(1)} %get-tuple-element.44.l_ref, bf16[48,5760]{1,0:T(8,128)(2,1)S(1)} %get-tuple-element.45.r_ref, bf16[640,5760]{1,0:T(8,128)(2,1)S(1)} %get-tuple-element.46.g_ref, ...), custom_call_target="tpu_custom_call", output_to_operand_aliasing={{0}: (4, {})} | custom-call | tf_op jit(solution)/shard_map/pallas_call | solution.py:215
  77.0 1.5 %shard_map.103 = (bf16[1,640,5760]{2,1,0:T(8,128)(2,1)}, f32[1,8,128]{2,1,0:T(8,128)S(1)}) custom-call(bf16[48,640]{1,0:T(8,128)(2,1)S(1)} %get-tuple-element.44.l_ref, bf16[48,5760]{1,0:T(8,128)(2,1)S(1)} %get-tuple-element.45.r_ref, bf16[640,5760]{1,0:T(8,128)(2,1)S(1)} %get-tuple-element.46.g_ref, ...), custom_call_target="tpu_custom_call", output_to_operand_aliasing={{0}: (4, {})} | custom-call | tf_op jit(solution)/shard_map/pallas_call | solution.py:215
  79.9 1.4 %shard_map.105 = (bf16[1,640,5760]{2,1,0:T(8,128)(2,1)}, f32[1,8,128]{2,1,0:T(8,128)S(1)}) custom-call(bf16[48,640]{1,0:T(8,128)(2,1)S(1)} %get-tuple-element.44.l_ref, bf16[48,5760]{1,0:T(8,128)(2,1)S(1)} %get-tuple-element.45.r_ref, bf16[640,5760]{1,0:T(8,128)(2,1)S(1)} %get-tuple-element.46.g_ref, ...), custom_call_target="tpu_custom_call", output_to_operand_aliasing={{0}: (4, {})} | custom-call | tf_op jit(solution)/shard_map/pallas_call | solution.py:215
  82.1 4.1 %collective-permute-start.24 = (f32[23,8,128]{2,1,0:T(8,128)S(1)}, f32[23,8,128]{2,1,0:T(8,128)S(1)}, u32[]{:S(2)}, u32[]{:S(2)}) collective-permute-start(f32[23,8,128]{2,1,0:T(8,128)S(1)} %shard_map.106.refs_0_), channel_id=1, source_target_pairs={{0,1},{1,0},{2,3},{3,2},{4,5},{5,4},{6,7},{7,6},{8,9},{9,8},{10,11... | collective-permute-start | bytes 282632 | tf_op jit(solution)/shard_map/ppermute | solution.py:36
  (65 shorter events, 24.7 us)
Async XLA Ops:
  7.4 4.2 %collective-permute-start.2 = (f32[125,8,128]{2,1,0:T(8,128)S(1)}, f32[125,8,128]{2,1,0:T(8,128)S(1)}, u32[]{:S(2)}, u32[]{:S(2)}) collective-permute-start(f32[125,8,128]{2,1,0:T(8,128)S(1)} %get-tuple-element.34.refs_2_), channel_id=1, source_target_pairs={{0,1},{1,0},{2,3},{3,2},{4,5},{5,4},{6,7},{7,6},{8,9},{9,8},{10,11... | collective-permute-start | bytes 1536008 | tf_op jit(solution)/shard_map/ppermute | solution.py:36
  8.9 2.6 %collective-permute-start = (f32[5,8,128]{2,1,0:T(8,128)S(1)}, f32[5,8,128]{2,1,0:T(8,128)S(1)}, u32[]{:S(2)}, u32[]{:S(2)}) collective-permute-start(f32[5,8,128]{2,1,0:T(8,128)S(1)} %get-tuple-element.33.refs_1_.refs_0_), channel_id=1, source_target_pairs={{0,2},{1,3},{2,0},{3,1},{4,6},{5,7},{6,4},{7,5},{8,10},{9,11},{10,... | collective-permute-start | bytes 61448 | tf_op jit(solution)/shard_map/ppermute | solution.py:32
  11.6 5.8 %collective-permute-start.4 = (f32[63,8,128]{2,1,0:T(8,128)S(1)}, f32[63,8,128]{2,1,0:T(8,128)S(1)}, u32[]{:S(2)}, u32[]{:S(2)}) collective-permute-start(f32[63,8,128]{2,1,0:T(8,128)S(1)} %get-tuple-element.36.refs_2_), channel_id=1, source_target_pairs={{0,32},{1,9},{2,34},{3,11},{4,36},{5,13},{6,38},{7,15},{8,40},{9,1... | collective-permute-start | bytes 774152 | tf_op jit(solution)/shard_map/ppermute | solution.py:32
  13.4 3.8 %collective-permute-start.1 = (f32[5,8,128]{2,1,0:T(8,128)S(1)}, f32[5,8,128]{2,1,0:T(8,128)S(1)}, u32[]{:S(2)}, u32[]{:S(2)}) collective-permute-start(f32[5,8,128]{2,1,0:T(8,128)S(1)} %shard_map.77.refs_2_.refs_0_), channel_id=1, source_target_pairs={{0,6},{1,7},{2,4},{3,5},{4,2},{5,3},{6,0},{7,1},{8,14},{9,15},{10,... | collective-permute-start | bytes 61448 | tf_op jit(solution)/shard_map/ppermute | solution.py:32
  17.4 3.9 %collective-permute-start.6 = (f32[32,8,128]{2,1,0:T(8,128)S(1)}, f32[32,8,128]{2,1,0:T(8,128)S(1)}, u32[]{:S(2)}, u32[]{:S(2)}) collective-permute-start(f32[32,8,128]{2,1,0:T(8,128)S(1)} %get-tuple-element.38.refs_2_), channel_id=1, source_target_pairs={{0,8},{1,3},{2,10},{3,1},{4,12},{5,7},{6,14},{7,5},{8,0},{9,11},{1... | collective-permute-start | bytes 393224 | tf_op jit(solution)/shard_map/ppermute | solution.py:32
  18.7 2.6 %collective-permute-start.3 = (f32[5,8,128]{2,1,0:T(8,128)S(1)}, f32[5,8,128]{2,1,0:T(8,128)S(1)}, u32[]{:S(2)}, u32[]{:S(2)}) collective-permute-start(f32[5,8,128]{2,1,0:T(8,128)S(1)} %shard_map.79.refs_2_.refs_0_), channel_id=1, source_target_pairs={{0,32},{1,33},{2,34},{3,35},{4,36},{5,37},{6,38},{7,39},{8,40},{9,... | collective-permute-start | bytes 61448 | tf_op jit(solution)/shard_map/ppermute | solution.py:32
  21.4 4.1 %collective-permute-start.8 = (f32[32,8,128]{2,1,0:T(8,128)S(1)}, f32[32,8,128]{2,1,0:T(8,128)S(1)}, u32[]{:S(2)}, u32[]{:S(2)}) collective-permute-start(f32[32,8,128]{2,1,0:T(8,128)S(1)} %shard_map.82.refs_2_.refs_0_), channel_id=1, source_target_pairs={{0,2},{1,33},{2,0},{3,35},{4,6},{5,37},{6,4},{7,39},{8,10},{9,41},... | collective-permute-start | bytes 393224 | tf_op jit(solution)/shard_map/ppermute | solution.py:32
  22.8 2.6 %collective-permute-start.5 = (f32[5,8,128]{2,1,0:T(8,128)S(1)}, f32[5,8,128]{2,1,0:T(8,128)S(1)}, u32[]{:S(2)}, u32[]{:S(2)}) collective-permute-start(f32[5,8,128]{2,1,0:T(8,128)S(1)} %shard_map.81.refs_2_.refs_0_), channel_id=1, source_target_pairs={{0,8},{1,9},{2,10},{3,11},{4,12},{5,13},{6,14},{7,15},{8,0},{9,1},... | collective-permute-start | bytes 61448 | tf_op jit(solution)/shard_map/ppermute | solution.py:32
  25.5 7.5 %collective-permute-start.10 = (f32[32,8,128]{2,1,0:T(8,128)S(1)}, f32[32,8,128]{2,1,0:T(8,128)S(1)}, u32[]{:S(2)}, u32[]{:S(2)}) collective-permute-start(f32[32,8,128]{2,1,0:T(8,128)S(1)} %shard_map.84.refs_2_.refs_0_), channel_id=1, source_target_pairs={{0,6},{1,97},{2,4},{3,99},{4,2},{5,101},{6,0},{7,103},{8,14},{9,10... | collective-permute-start | bytes 393224 | tf_op jit(solution)/shard_map/ppermute | solution.py:32
  28.4 4.6 %collective-permute-start.7 = (f32[5,8,128]{2,1,0:T(8,128)S(1)}, f32[5,8,128]{2,1,0:T(8,128)S(1)}, u32[]{:S(2)}, u32[]{:S(2)}) collective-permute-start(f32[5,8,128]{2,1,0:T(8,128)S(1)} %shard_map.83.refs_2_.refs_0_), channel_id=1, source_target_pairs={{0,16},{1,17},{2,18},{3,19},{4,20},{5,21},{6,22},{7,23},{8,24},{9,... | collective-permute-start | bytes 61448 | tf_op jit(solution)/shard_map/ppermute | solution.py:32
  33.0 3.8 %collective-permute-start.9 = (f32[5,8,128]{2,1,0:T(8,128)S(1)}, f32[5,8,128]{2,1,0:T(8,128)S(1)}, u32[]{:S(2)}, u32[]{:S(2)}) collective-permute-start(f32[5,8,128]{2,1,0:T(8,128)S(1)} %shard_map.85.refs_2_.refs_0_), channel_id=1, source_target_pairs={{0,96},{1,97},{2,98},{3,99},{4,100},{5,101},{6,102},{7,103},{8,104... | collective-permute-start | bytes 61448 | tf_op jit(solution)/shard_map/ppermute | solution.py:32
  33.1 16.5 %collective-permute-start.14 = (f32[32,8,128]{2,1,0:T(8,128)S(1)}, f32[32,8,128]{2,1,0:T(8,128)S(1)}, u32[]{:S(2)}, u32[]{:S(2)}) collective-permute-start(f32[32,8,128]{2,1,0:T(8,128)S(1)} %shard_map.86.refs_2_.refs_0_), channel_id=1, source_target_pairs={{0,16},{1,7},{2,18},{3,5},{4,20},{5,3},{6,22},{7,1},{8,24},{9,15},... | collective-permute-start | bytes 393224 | tf_op jit(solution)/shard_map/ppermute | solution.py:32
  36.8 9.4 %collective-permute-start.11 = (f32[5,8,128]{2,1,0:T(8,128)S(1)}, f32[5,8,128]{2,1,0:T(8,128)S(1)}, u32[]{:S(2)}, u32[]{:S(2)}) collective-permute-start(f32[5,8,128]{2,1,0:T(8,128)S(1)} %shard_map.87.refs_0_), channel_id=1, source_target_pairs={{0,1},{1,0},{2,3},{3,2},{4,5},{5,4},{6,7},{7,6},{8,9},{9,8},{10,11... | collective-permute-start | bytes 61448 | tf_op jit(solution)/shard_map/ppermute | solution.py:36
  49.6 6.4 %collective-permute-start.15 = (f32[32,8,128]{2,1,0:T(8,128)S(1)}, f32[32,8,128]{2,1,0:T(8,128)S(1)}, u32[]{:S(2)}, u32[]{:S(2)}) collective-permute-start(f32[32,8,128]{2,1,0:T(8,128)S(1)} %shard_map.91.refs_2_.refs_0_), channel_id=1, source_target_pairs={{0,96},{1,17},{2,98},{3,19},{4,100},{5,21},{6,102},{7,23},{8,104},... | collective-permute-start | bytes 393224 | tf_op jit(solution)/shard_map/ppermute | solution.py:32
  51.3 4.6 %collective-permute-start.13 = (f32[23,8,128]{2,1,0:T(8,128)S(1)}, f32[23,8,128]{2,1,0:T(8,128)S(1)}, u32[]{:S(2)}, u32[]{:S(2)}) collective-permute-start(f32[23,8,128]{2,1,0:T(8,128)S(1)} %shard_map.90.refs_2_.refs_0_), channel_id=1, source_target_pairs={{0,2},{1,7},{2,0},{3,5},{4,6},{5,3},{6,4},{7,1},{8,10},{9,15},{10,... | collective-permute-start | bytes 282632 | tf_op jit(solution)/shard_map/ppermute | solution.py:32
  56.0 4.8 %collective-permute-start.17 = (f32[32,8,128]{2,1,0:T(8,128)S(1)}, f32[32,8,128]{2,1,0:T(8,128)S(1)}, u32[]{:S(2)}, u32[]{:S(2)}) collective-permute-start(f32[32,8,128]{2,1,0:T(8,128)S(1)} %shard_map.93.rest_1_.refs_0_), channel_id=1, source_target_pairs={{0,8},{1,3},{2,10},{3,1},{4,12},{5,7},{6,14},{7,5},{8,0},{9,11},{1... | collective-permute-start | bytes 393224 | tf_op jit(solution)/shard_map/ppermute | solution.py:32
  56.1 4.7 %collective-permute-start.16 = (f32[23,8,128]{2,1,0:T(8,128)S(1)}, f32[23,8,128]{2,1,0:T(8,128)S(1)}, u32[]{:S(2)}, u32[]{:S(2)}) collective-permute-start(f32[23,8,128]{2,1,0:T(8,128)S(1)} %shard_map.92.refs_2_.rest_0_.refs_0_), channel_id=1, source_target_pairs={{0,32},{1,97},{2,34},{3,99},{4,36},{5,101},{6,38},{7,103},{8,40},{... | collective-permute-start | bytes 282632 | tf_op jit(solution)/shard_map/ppermute | solution.py:32
  60.9 5.6 %collective-permute-start.19 = (f32[63,8,128]{2,1,0:T(8,128)S(1)}, f32[63,8,128]{2,1,0:T(8,128)S(1)}, u32[]{:S(2)}, u32[]{:S(2)}) collective-permute-start(f32[63,8,128]{2,1,0:T(8,128)S(1)} %shard_map.96.rest_2_.refs_0_), channel_id=1, source_target_pairs={{0,32},{1,9},{2,34},{3,11},{4,36},{5,13},{6,38},{7,15},{8,40},{9,1... | collective-permute-start | bytes 774152 | tf_op jit(solution)/shard_map/ppermute | solution.py:32
  61.1 3.7 %collective-permute-start.18 = (f32[23,8,128]{2,1,0:T(8,128)S(1)}, f32[23,8,128]{2,1,0:T(8,128)S(1)}, u32[]{:S(2)}, u32[]{:S(2)}) collective-permute-start(f32[23,8,128]{2,1,0:T(8,128)S(1)} %shard_map.95.refs_2_.rest_1_.refs_0_), channel_id=1, source_target_pairs={{0,6},{1,3},{2,4},{3,1},{4,2},{5,7},{6,0},{7,5},{8,14},{9,11},{10,... | collective-permute-start | bytes 282632 | tf_op jit(solution)/shard_map/ppermute | solution.py:32
  66.5 8.3 %collective-permute-start.21 = (f32[125,8,128]{2,1,0:T(8,128)S(1)}, f32[125,8,128]{2,1,0:T(8,128)S(1)}, u32[]{:S(2)}, u32[]{:S(2)}) collective-permute-start(f32[125,8,128]{2,1,0:T(8,128)S(1)} %shard_map.99.rest_2_.refs_0_), channel_id=1, source_target_pairs={{0,1},{1,0},{2,3},{3,2},{4,5},{5,4},{6,7},{7,6},{8,9},{9,8},{10,11... | collective-permute-start | bytes 1536008 | tf_op jit(solution)/shard_map/ppermute | solution.py:36
  68.2 5.3 %collective-permute-start.20 = (f32[23,8,128]{2,1,0:T(8,128)S(1)}, f32[23,8,128]{2,1,0:T(8,128)S(1)}, u32[]{:S(2)}, u32[]{:S(2)}) collective-permute-start(f32[23,8,128]{2,1,0:T(8,128)S(1)} %shard_map.98.refs_2_.rest_1_.refs_0_), channel_id=1, source_target_pairs={{0,8},{1,17},{2,10},{3,19},{4,12},{5,21},{6,14},{7,23},{8,0},{9,25... | collective-permute-start | bytes 282632 | tf_op jit(solution)/shard_map/ppermute | solution.py:32
  73.5 5.0 %collective-permute-start.22 = (f32[23,8,128]{2,1,0:T(8,128)S(1)}, f32[23,8,128]{2,1,0:T(8,128)S(1)}, u32[]{:S(2)}, u32[]{:S(2)}) collective-permute-start(f32[23,8,128]{2,1,0:T(8,128)S(1)} %shard_map.101.refs_2_.rest_1_.refs_0_), channel_id=1, source_target_pairs={{0,96},{1,33},{2,98},{3,35},{4,100},{5,37},{6,102},{7,39},{8,104},... | collective-permute-start | bytes 282632 | tf_op jit(solution)/shard_map/ppermute | solution.py:32
  78.5 3.5 %collective-permute-start.23 = (f32[23,8,128]{2,1,0:T(8,128)S(1)}, f32[23,8,128]{2,1,0:T(8,128)S(1)}, u32[]{:S(2)}, u32[]{:S(2)}) collective-permute-start(f32[23,8,128]{2,1,0:T(8,128)S(1)} %shard_map.104.rest_1_.refs_0_), channel_id=1, source_target_pairs={{0,16},{1,9},{2,18},{3,11},{4,20},{5,13},{6,22},{7,15},{8,24},{9,1... | collective-permute-start | bytes 282632 | tf_op jit(solution)/shard_map/ppermute | solution.py:32
  82.1 5.0 %collective-permute-start.24 = (f32[23,8,128]{2,1,0:T(8,128)S(1)}, f32[23,8,128]{2,1,0:T(8,128)S(1)}, u32[]{:S(2)}, u32[]{:S(2)}) collective-permute-start(f32[23,8,128]{2,1,0:T(8,128)S(1)} %shard_map.106.refs_0_), channel_id=1, source_target_pairs={{0,1},{1,0},{2,3},{3,2},{4,5},{5,4},{6,7},{7,6},{8,9},{9,8},{10,11... | collective-permute-start | bytes 282632 | tf_op jit(solution)/shard_map/ppermute | solution.py:36
  (4 other events, 12.0 us)

commit v2 on v1

v2 whole, which is shorter than its diff:
```python
import jax
import jax.numpy as jnp
from jax import lax
from jax.experimental import pallas as pl
from jax.experimental.pallas import tpu as pltpu
from jax.sharding import PartitionSpec as P

AXES = ("row", "col")
MIB = 1 << 20
LANES = 128
SUBS = 8
F32 = jnp.float32
BF16 = jnp.bfloat16
RING_BIT = {"x": 1, "z": 3, "y": 5}
AROUND = ("x", "y", "z")
P_HOPS = (("x0", "x1", "y0", "y1", "z1", "z0"), ("y0", "y1", "z0", "z1", "x1", "x0"))
Q_HOPS = (("x1", "z1", "z0", "y0", "x0", "y1"), ("y1", "x1", "x0", "z0", "y0", "z1"))
HALVINGS = (0, 2)
SLABS = (1, 0, 3, 0, 0, 1)
LAST_PARTS = 3
SHORT = pl.CostEstimate(flops=0, bytes_accessed=0, transcendentals=0)
LONG = pl.CostEstimate(flops=10_000_000_000, bytes_accessed=0, transcendentals=0)


def partner(index, hops):
    ring, level = hops[index & 1]
    bit = RING_BIT[ring]
    if level == "0":
        return index ^ (1 << bit)
    return index ^ ((3 if ring in AROUND else 2) << bit)


def swap(x, hops, step):
    pair = (hops[0][step], hops[1][step])
    return lax.ppermute(x, AXES, [(i, partner(i, pair)) for i in range(lax.axis_size(AXES))])


def swap_cores(x):
    return lax.ppermute(x, AXES, [(i, i ^ 1) for i in range(lax.axis_size(AXES))])


def place():
    return lax.axis_index("row") * lax.axis_size("col") + lax.axis_index("col")


def keeps_high(index, halving):
    def of(hop):
        bit = RING_BIT[hop[0]]
        low, high = (index >> bit) & 1, (index >> (bit + 1)) & 1
        if hop[1] == "1":
            return high
        return low ^ high if hop[0] in AROUND else low

    core = index & 1
    step = HALVINGS[halving]
    return jnp.where(core == 0, of(P_HOPS[0][step]), of(P_HOPS[1][step])) == 1


def in_hbm(x):
    return pltpu.with_memory_space_constraint(x, pltpu.HBM)


def blocks(count):
    return jax.ShapeDtypeStruct((count, SUBS, LANES), F32)


def call(body, operands, outs, after=(), cost=SHORT, limit=12):
    count = len(operands)

    def kernel(*refs):
        body(*refs[:count], *refs[count + len(after) :])

    return pl.pallas_call(
        kernel,
        in_specs=[pl.BlockSpec(memory_space=pltpu.VMEM)] * count + [pl.BlockSpec(memory_space=pl.ANY)] * len(after),
        out_specs=jax.tree.map(lambda _: pl.BlockSpec(memory_space=pltpu.VMEM), outs),
        out_shape=outs,
        compiler_params=pltpu.CompilerParams(vmem_limit_bytes=limit * MIB),
        cost_estimate=cost,
    )(*operands, *after)


def left_product(grads, residuals, q_rows):
    _, rows, cols = grads.shape
    rank = q_rows.shape[0]
    parts = rows // LANES

    wide = cols // LAST_PARTS
    pieces = [(i, 0, cols) for i in range(parts - 1)]
    pieces += [(parts - 1, j * wide, wide) for j in range(LAST_PARTS)]

    def body(g_hbm, r_hbm, q_hbm, p_ref, c_ref, g_ref, r_ref, q_ref, sems):
        copies = [pltpu.make_async_copy(q_hbm, q_ref, sems.at[2 * len(pieces)])]
        for n, (i, first, width) in enumerate(pieces):
            own = (pl.ds(i * LANES, LANES), pl.ds(first, width))
            copies.append(pltpu.make_async_copy(g_hbm.at[(0, *own)], g_ref.at[own], sems.at[2 * n]))
            copies.append(pltpu.make_async_copy(r_hbm.at[(0, *own)], r_ref.at[own], sems.at[2 * n + 1]))
        for copy in copies:
            copy.start()
        copies[0].wait()
        for n, (i, first, width) in enumerate(pieces):
            own = (slice(i * LANES, (i + 1) * LANES), slice(first, first + width))
            copies[2 * n + 1].wait()
            copies[2 * n + 2].wait()
            compensated = (g_ref[own].astype(F32) + r_ref[own].astype(F32)).astype(BF16)
            c_ref[own] = compensated
            part = lax.dot_general(
                q_ref[:, own[1]].astype(BF16),
                compensated,
                (((1,), (1,)), ((), ())),
                preferred_element_type=F32,
            )
            p_ref[i] = part if first == 0 else p_ref[i] + part

    whole = pltpu.VMEM((rows, cols), BF16)
    return pl.pallas_call(
        body,
        in_specs=[pl.BlockSpec(memory_space=pltpu.HBM)] * 3,
        out_specs=[pl.BlockSpec(memory_space=pltpu.VMEM)] * 4,
        out_shape=[blocks(parts), whole, whole, whole],
        scratch_shapes=[pltpu.VMEM((rank, cols), F32), pltpu.SemaphoreType.DMA((2 * len(pieces) + 1,))],
        compiler_params=pltpu.CompilerParams(vmem_limit_bytes=32 * MIB),
    )(in_hbm(grads), in_hbm(residuals), in_hbm(q_rows))


def product_tiles(half, c_ref, first, out_ref):
    count = out_ref.shape[0]
    for t in range(0, count, 8):
        width = min(8, count - t) * LANES
        here = pl.ds(pl.multiple_of((first + t) * LANES, LANES), width)
        part = lax.dot_general(half, c_ref[:, here], (((1,), (0,)), ((), ())), preferred_element_type=F32)
        for k in range(width // LANES):
            out_ref[t + k] = part[:, k * LANES : (k + 1) * LANES]


def right_product(p_tiles, p_other, compensated):
    tiles, rank, _ = p_tiles.shape
    rows, cols = compensated.shape
    out_tiles = cols // LANES
    count = (out_tiles + 1) // 2

    def body(p_ref, o_ref, c_ref, orth_ref, send_ref):
        total = jnp.concatenate([p_ref[t] + o_ref[t] for t in range(tiles)], axis=1)
        gram = lax.dot_general(
            total, total, (((1,), (1,)), ((), ())), precision=lax.Precision.HIGHEST, preferred_element_type=F32
        )
        sub = lax.broadcasted_iota(jnp.int32, (rank, 1), 0)
        for j in range(rank):
            scale = lax.rsqrt(gram[j : j + 1, j : j + 1])
            column = jnp.where(sub > j, gram[:, j : j + 1] * scale, 0.0)
            gram_row, total_row = gram[j : j + 1, :] * scale, total[j : j + 1, :] * scale
            gram = jnp.where(sub == j, gram_row, gram - column * gram_row)
            total = jnp.where(sub == j, total_row, total - column * total_row)
        orth_ref[...] = total
        first = jnp.where(place() & 1 == 0, out_tiles - count, 0)
        product_tiles(total.astype(BF16), c_ref, first, send_ref)

    outs = [jax.ShapeDtypeStruct((rank, rows), F32), blocks(count)]
    return call(body, [p_tiles, p_other, compensated], outs)


def own_product(orth, compensated, after):
    out_tiles = compensated.shape[1] // LANES
    count = (out_tiles + 1) // 2

    def body(orth_ref, c_ref, keep_ref):
        first = jnp.where(place() & 1 == 0, 0, out_tiles - count)
        product_tiles(orth_ref[...].astype(BF16), c_ref, first, keep_ref)

    return call(body, [orth, compensated], blocks(count), after, LONG)


def thirds(x):
    a = x.astype(BF16)
    rest = x - a.astype(F32)
    b = rest.astype(BF16)
    return a, b, (rest - b.astype(F32)).astype(BF16)


def factors(orth, q_keep, q_send, own_rows, tiles):
    rank, rows = orth.shape
    count = q_keep.shape[0]

    def body(p_ref, keep_ref, send_ref, left_ref, right_ref, own_ref):
        a, b, c = thirds(p_ref[...])
        left_ref[...] = jnp.concatenate([a, a, b, a, b, c], axis=0)

        def write(low_ref, high_ref):
            for t in range(tiles):
                a, b, c = thirds(low_ref[t] if t < count else high_ref[t - tiles + count])
                right_ref[:, t * LANES : (t + 1) * LANES] = jnp.concatenate([a, b, a, c, b, a], axis=0)

        core = place() & 1

        @pl.when(core == 0)
        def _():
            write(keep_ref, send_ref)

        @pl.when(core == 1)
        def _():
            write(send_ref, keep_ref)

        column = lax.broadcasted_iota(jnp.int32, (SUBS, rows), 1)
        row = lax.broadcasted_iota(jnp.int32, (SUBS, rows), 0)
        chosen = jnp.where(column == place() * own_rows + row, 1.0, 0.0)
        own_ref[...] = lax.dot_general(
            chosen, p_ref[...], (((1,), (1,)), ((), ())), precision=lax.Precision.HIGHEST, preferred_element_type=F32
        )

    outs = [
        jax.ShapeDtypeStruct((6 * rank, rows), BF16),
        jax.ShapeDtypeStruct((6 * rank, tiles * LANES), BF16),
        jax.ShapeDtypeStruct((SUBS, rank), F32),
    ]
    return call(body, [orth, q_keep, q_send], outs, cost=LONG)


def residual_rows(first, count, left, right, grads, residuals, before, after):
    rows, cols = grads.shape
    step = 9 * LANES
    parts = cols // step
    own = slice(first * LANES, (first + count) * LANES)

    def body(l_ref, r_ref, g_ref, e_ref, *rest):
        out_hbm, done_ref, stage, sems = rest[-4:]
        copies = []
        for j in range(parts):
            here = slice(j * step, (j + 1) * step)
            wide = g_ref[own, here].astype(F32) + e_ref[own, here].astype(F32)
            away = lax.dot_general(
                l_ref[:, own], r_ref[:, here], (((0,), (0,)), ((), ())), preferred_element_type=F32
            )
            stage[:, here] = (wide - away).astype(BF16)
            copies.append(
                pltpu.make_async_copy(stage.at[:, here], out_hbm.at[0, own, here], sems.at[j])
            )
            copies[-1].start()
        done_ref[...] = jnp.zeros_like(done_ref)
        for copy in copies:
            copy.wait()

    operands = [left, right, grads, residuals]
    vmem, anywhere = pl.BlockSpec(memory_space=pltpu.VMEM), pl.BlockSpec(memory_space=pl.ANY)
    others = ([] if before is None else [before]) + list(after)
    return pl.pallas_call(
        body,
        in_specs=[vmem] * 4 + [anywhere] * len(others),
        out_specs=[pl.BlockSpec(memory_space=pltpu.HBM), vmem],
        out_shape=[jax.ShapeDtypeStruct((1, rows, cols), BF16), blocks(1)],
        scratch_shapes=[pltpu.VMEM((count * LANES, cols), BF16), pltpu.SemaphoreType.DMA((parts,))],
        input_output_aliases={} if before is None else {4: 0},
        compiler_params=pltpu.CompilerParams(vmem_limit_bytes=12 * MIB),
        cost_estimate=LONG,
    )(*operands, *others)


def add(a, b, after=(), cost=SHORT):
    def body(a_ref, b_ref, out_ref):
        out_ref[...] = a_ref[...] + b_ref[...]

    return call(body, [a, b], blocks(a.shape[0]), after, cost)


def hold(x, after):
    def body(x_ref, out_ref):
        out_ref[...] = x_ref[...]

    return call(body, [x], blocks(x.shape[0]), after, LONG)


def marker(after):
    def body(out_ref):
        out_ref[...] = jnp.zeros_like(out_ref)

    return call(body, [], blocks(1), after, LONG)


def first_half(vec, other, after):
    height, width = vec.shape
    across = width // LANES
    half = height // SUBS * across // 2
    part = (half + 1) // 2

    def body(vec_ref, other_ref, keep_ref, send_ref):
        def copy(first, out_ref):
            for t in range(part):
                y, x = (first + t) // across * SUBS, (first + t) % across * LANES
                here = (slice(y, y + SUBS), slice(x, x + LANES))
                out_ref[t] = vec_ref[here] + other_ref[here]

        index = place()
        high = keeps_high(index, 0)
        for core in (0, 1):
            for up in (False, True):
                low_ref, high_ref = (send_ref, keep_ref) if up else (keep_ref, send_ref)

                @pl.when((index & 1 == core) & (high if up else ~high))
                def _(core=core, low_ref=low_ref, high_ref=high_ref):
                    copy(core * half, low_ref)
                    copy(core * half + half - part, high_ref)

    return call(body, [vec, other], [blocks(part), blocks(part)], after, LONG)


def halve(halving, a, b, after):
    size = a.shape[0]
    part = (size + 1) // 2

    def body(a_ref, b_ref, keep_ref, send_ref):
        low = a_ref[:part] + b_ref[:part]
        high = a_ref[size - part :] + b_ref[size - part :]
        flag = keeps_high(place(), halving)
        keep_ref[...] = jnp.where(flag, high, low)
        send_ref[...] = jnp.where(flag, low, high)

    return call(body, [a, b], [blocks(part), blocks(part)], after, LONG)


def join(halving, size, mine, other, after):
    part = mine.shape[0]

    def body(mine_ref, other_ref, out_ref):
        flag = keeps_high(place(), halving)
        mine, other = mine_ref[...], other_ref[...]
        out_ref[size - part :] = jnp.where(flag, mine, other)
        out_ref[:part] = jnp.where(flag, other, mine)

    return call(body, [mine, other], blocks(size), after, LONG)


def join_vectors(mine, other, shape, replicas, after):
    across = shape[1] // LANES
    half = mine.shape[0]

    def body(mine_ref, other_ref, vec_ref, done_ref):
        done_ref[...] = jnp.zeros_like(done_ref)

        def write(low_ref, high_ref):
            for t in range(2 * half):
                y, x = t // across * SUBS, t % across * LANES
                tile = low_ref[t] if t < half else high_ref[t - half]
                vec_ref[y : y + SUBS, x : x + LANES] = tile * (1.0 / replicas)

        core = place() & 1

        @pl.when(core == 0)
        def _():
            write(mine_ref, other_ref)

        @pl.when(core == 1)
        def _():
            write(other_ref, mine_ref)

    return call(body, [mine, other], [jax.ShapeDtypeStruct(shape, F32), blocks(1)], after, LONG)


def finish(mine, other, own, own_rows, tiles, replicas, after):
    count, rank, _ = mine.shape

    def body(mine_ref, other_ref, own_ref, q_ref, d_ref):
        def write(low_ref, high_ref):
            columns = [own_ref[:own_rows, k : k + 1] for k in range(rank)]
            for t in range(tiles):
                mean = (low_ref[t] if t < count else high_ref[t - tiles + count]) * (1.0 / replicas)
                q_ref[:, t * LANES : (t + 1) * LANES] = mean
                out = columns[0] * mean[0:1, :]
                for k in range(1, rank):
                    out = out + columns[k] * mean[k : k + 1, :]
                d_ref[:, t * LANES : (t + 1) * LANES] = out

        core = place() & 1

        @pl.when(core == 0)
        def _():
            write(mine_ref, other_ref)

        @pl.when(core == 1)
        def _():
            write(other_ref, mine_ref)

    outs = [
        jax.ShapeDtypeStruct((rank, tiles * LANES), F32),
        jax.ShapeDtypeStruct((own_rows, tiles * LANES), F32),
    ]
    return call(body, [mine, other, own], outs, after)


def on_device(grads, residuals, q_prev, vec_grads):
    devices = lax.axis_size(AXES)
    steps = len(P_HOPS[0])
    tiles = grads.shape[2] // LANES
    own_rows = grads.shape[1] // devices
    half = vec_grads.size // (2 * SUBS * LANES)
    sizes = [half]
    for _ in HALVINGS:
        sizes.append((sizes[-1] + 1) // 2)
    v_other = swap_cores(vec_grads)
    p, compensated, g_here, r_here = left_product(grads, residuals, q_prev.T)

    v_keep = v_send = v_got = None
    for step in range(steps):
        got = swap(p, P_HOPS, step)
        after = []
        if step != 1:
            if step == 0:
                v_keep, v_send = first_half(vec_grads, v_other, [p])
            elif step in HALVINGS:
                v_keep, v_send = halve(HALVINGS.index(step), v_keep, v_got, [p])
            elif step < steps - 1:
                v_keep = v_send = add(v_keep, v_got, [p], LONG)
            else:
                v_keep = v_send = hold(v_keep, [p])
            if step != 4:
                v_got = swap(v_send, P_HOPS, step)
            after = [marker([v_send])]
        p = add(p, got, after)

    orth, q_send = right_product(p, swap_cores(p), compensated)
    got = swap_cores(q_send)
    q_keep = own_product(orth, compensated, [q_send])
    left, right, own = factors(orth, q_keep, q_send, own_rows, tiles)
    q = add(q_keep, got, [left])
    fresh = None
    for step in range(steps):
        got = swap(q, Q_HOPS, step)
        after = [q]
        if step == steps - 1:
            fresh, done = residual_rows(sum(SLABS[:step]), SLABS[step], left, right, g_here, r_here, fresh, after)
            after = [done]
        if step in (0, 1, 3):
            v_keep = add(v_keep, v_got, after, LONG)
        elif step > 3:
            v_keep = join(steps - 1 - step, sizes[steps - 1 - step], v_keep, v_got, after)
        if step != 2:
            v_got = swap(v_keep, Q_HOPS, step) if step < steps - 1 else swap_cores(v_keep)
        if SLABS[step] and step < steps - 1:
            fresh, done = residual_rows(
                sum(SLABS[:step]), SLABS[step], left, right, g_here, r_here, fresh, [q, v_keep]
            )
        else:
            done = marker([q, v_keep])
        q = add(q, got, [done])

    other = swap_cores(q)
    vec_mean, done = join_vectors(v_keep, v_got, vec_grads.shape, devices, [q])
    q_next, decompressed = finish(q, other, own, own_rows, tiles, devices, [done])
    return (fresh, decompressed, q_next.T, vec_mean)


def solution(mesh):
    return jax.shard_map(
        on_device,
        mesh=mesh,
        in_specs=(P(AXES, None, None), P(AXES, None, None), P(), P(AXES, None)),
        out_specs=(P(AXES, None, None), P(AXES, None), P(), P()),
        check_vma=False,
    )
```

time: 88.2 us -> 77.2 us (0.88)
  starting transfers between devices: 48.4 us -> 44 us
  waiting for transfers between devices: 19 us -> 15.4 us
  Pallas kernels: 18.5 us -> 16.9 us
  local copies, waits for them, and re-layouts: 1.22 us -> 0.01 us
    ppermute x20, starting transfers between devices: 32.2 us -> 28.7 us  [swap(): lax.ppermute(x, AXES, [(i, partner(i, pair)) for i in range(lax.axis_size...]
    ppermute x20, waiting for transfers between devices: 16.5 us -> 14 us  [swap(): lax.ppermute(x, AXES, [(i, partner(i, pair)) for i in range(lax.axis_size...]
    pallas_call x5 -> x3, Pallas kernels: 7.23 us -> 5.47 us  [residual_rows(): pl.pallas_call(body, in_specs=[vmem] * 4 + [anywhere] * len(others), out_...]
    unnamed x6 -> x2, local copies, waits for them, and re-layouts: 1.22 us -> 0.01 us
    ppermute x5, waiting for transfers between devices: 2.51 us -> 1.42 us  [swap_cores(): lax.ppermute(x, AXES, [(i, i ^ 1) for i in range(lax.axis_size(AXES))])]
    ppermute x5, starting transfers between devices: 16.2 us -> 15.2 us  [swap_cores(): lax.ppermute(x, AXES, [(i, i ^ 1) for i in range(lax.axis_size(AXES))])]
    pallas_call x27 -> x37, Pallas kernels: 4.67 us -> 4.7 us  [call(): pl.pallas_call(kernel, in_specs=[pl.BlockSpec(memory_space=pltpu.VMEM)] *...]
  transfers between devices with their start and end apart: 25 -> 25, of which waited for: 17 -> 15; matrix products, arithmetic and copies ran while one was open for 0% -> 0% of each run, Pallas kernels for 12% -> 21%
where the time goes in v2:
time: 77.2 us; the launch traced here: 77.1 us
  starting transfers between devices  44 us (57%)
  Pallas kernels  16.9 us (22%)
  waiting for transfers between devices  15.4 us (20%)
  between operations  0.79 us (1%)
    ppermute x20, starting transfers between devices, swap(): lax.ppermute(x, AXES, [(i, partner(i, pair)) for i in range(lax.axis_size...  28.7 us
    ppermute x5, starting transfers between devices, swap_cores(): lax.ppermute(x, AXES, [(i, i ^ 1) for i in range(lax.axis_size(AXES))])  15.2 us
    ppermute x20, waiting for transfers between devices, swap(): lax.ppermute(x, AXES, [(i, partner(i, pair)) for i in range(lax.axis_size...  14 us
    pallas_call x1, Pallas kernels, left_product(): pl.pallas_call(body, in_specs=[pl.BlockSpec(memory_space=pltpu.HBM)] * 3,...  6.7 us
    pallas_call x3, Pallas kernels, residual_rows(): pl.pallas_call(body, in_specs=[vmem] * 4 + [anywhere] * len(others), out_...  5.47 us
    pallas_call x37, Pallas kernels, call(): pl.pallas_call(kernel, in_specs=[pl.BlockSpec(memory_space=pltpu.VMEM)] *...  4.7 us
  transfers between devices with their start and end apart: 25, of which 15 were waited for; matrix products, arithmetic and copies ran while one was open for 0% of the time, Pallas kernels for 21%

profile of v2, /device:TPU:1, one launch (start us, length us, event | category | flops | bytes accessed | tf_op | source)
XLA Modules:
  0.0 77.1 jit_solution(17735139717533012318)
XLA Ops:
  0.6 1.5 %collective-permute-start.1 = (f32[200,1280]{1,0:T(8,128)}, f32[200,1280]{1,0:T(8,128)S(1)}, u32[]{:S(2)}, u32[]{:S(2)}) collective-permute-start(f32[200,1280]{1,0:T(8,128)} %refs_0_.1), channel_id=1, source_target_pairs={{0,1},{1,0},{2,3},{3,2},{4,5},{5,4},{6,7},{7,6},{8,9},{9,8},{10,11... | collective-permute-start | bytes 3072008 | tf_op jit(solution)/shard_map/ppermute | solution.py:39
  2.1 6.7 %shard_map.75 = (f32[5,8,128]{2,1,0:T(8,128)S(1)}, bf16[640,5760]{1,0:T(8,128)(2,1)S(1)}, bf16[640,5760]{1,0:T(8,128)(2,1)S(1)}, bf16[640,5760]{1,0:T(8,128)(2,1)S(1)}) custom-call(bf16[1,640,5760]{2,1,0:T(8,128)(2,1)} %g_hbm.1, bf16[1,640,5760]{2,1,0:T(8,128)(2,1)} %r_hbm.1, f32[8,5760]{1,0:T(8,128)} %bitcast.2), custom_call_target="tpu_custom_call" | custom-call | tf_op jit(solution)/shard_map/pallas_call | solution.py:116
  8.8 1.5 %collective-permute-start = (f32[5,8,128]{2,1,0:T(8,128)S(1)}, f32[5,8,128]{2,1,0:T(8,128)S(1)}, u32[]{:S(2)}, u32[]{:S(2)}) collective-permute-start(f32[5,8,128]{2,1,0:T(8,128)S(1)} %get-tuple-element.27.refs_2_.refs_0_), channel_id=1, source_target_pairs={{0,2},{1,33},{2,0},{3,35},{4,6},{5,37},{6,4},{7,39},{8,10},{9,41},... | collective-permute-start | bytes 61448 | tf_op jit(solution)/shard_map/ppermute | solution.py:35
  11.6 2.8 %collective-permute-start.2 = (f32[5,8,128]{2,1,0:T(8,128)S(1)}, f32[5,8,128]{2,1,0:T(8,128)S(1)}, u32[]{:S(2)}, u32[]{:S(2)}) collective-permute-start(f32[5,8,128]{2,1,0:T(8,128)S(1)} %shard_map.78.refs_0_), channel_id=1, source_target_pairs={{0,6},{1,97},{2,4},{3,99},{4,2},{5,101},{6,0},{7,103},{8,14},{9,10... | collective-permute-start | bytes 61448 | tf_op jit(solution)/shard_map/ppermute | solution.py:35
  14.4 1.2 %collective-permute-done.2.refs_1_ = f32[5,8,128]{2,1,0:T(8,128)S(1)} collective-permute-done((f32[5,8,128]{2,1,0:T(8,128)S(1)}, f32[5,8,128]{2,1,0:T(8,128)S(1)}, u32[]{:S(2)}, u32[]{:S(2)}) %collective-permute-start.2) | collective-permute-done | bytes 20512 | tf_op jit(solution)/shard_map/ppermute | solution.py:35
  15.6 1.6 %collective-permute-start.3 = (f32[5,8,128]{2,1,0:T(8,128)S(1)}, f32[5,8,128]{2,1,0:T(8,128)S(1)}, u32[]{:S(2)}, u32[]{:S(2)}) collective-permute-start(f32[5,8,128]{2,1,0:T(8,128)S(1)} %shard_map.79.refs_2_.refs_0_), channel_id=1, source_target_pairs={{0,32},{1,9},{2,34},{3,11},{4,36},{5,13},{6,38},{7,15},{8,40},{9,1... | collective-permute-start | bytes 61448 | tf_op jit(solution)/shard_map/ppermute | solution.py:35
  18.4 3.6 %collective-permute-start.5 = (f32[5,8,128]{2,1,0:T(8,128)S(1)}, f32[5,8,128]{2,1,0:T(8,128)S(1)}, u32[]{:S(2)}, u32[]{:S(2)}) collective-permute-start(f32[5,8,128]{2,1,0:T(8,128)S(1)} %shard_map.82.refs_2_.refs_0_), channel_id=1, source_target_pairs={{0,96},{1,25},{2,98},{3,27},{4,100},{5,29},{6,102},{7,31},{8,104},... | collective-permute-start | bytes 61448 | tf_op jit(solution)/shard_map/ppermute | solution.py:35
  22.0 1.8 %collective-permute-start.8 = (f32[32,8,128]{2,1,0:T(8,128)S(1)}, f32[32,8,128]{2,1,0:T(8,128)S(1)}, u32[]{:S(2)}, u32[]{:S(2)}) collective-permute-start(f32[32,8,128]{2,1,0:T(8,128)S(1)} %shard_map.83.refs_0_), channel_id=1, source_target_pairs={{0,96},{1,25},{2,98},{3,27},{4,100},{5,29},{6,102},{7,31},{8,104},... | collective-permute-start | bytes 393224 | tf_op jit(solution)/shard_map/ppermute | solution.py:35
  23.8 2.6 %collective-permute-start.7 = (f32[5,8,128]{2,1,0:T(8,128)S(1)}, f32[5,8,128]{2,1,0:T(8,128)S(1)}, u32[]{:S(2)}, u32[]{:S(2)}) collective-permute-start(f32[5,8,128]{2,1,0:T(8,128)S(1)} %shard_map.85.refs_2_.refs_0_), channel_id=1, source_target_pairs={{0,24},{1,7},{2,26},{3,5},{4,28},{5,3},{6,30},{7,1},{8,16},{9,15},... | collective-permute-start | bytes 61448 | tf_op jit(solution)/shard_map/ppermute | solution.py:35
  28.5 2.1 %collective-permute-done.9.refs_1_ = f32[5,8,128]{2,1,0:T(8,128)S(1)} collective-permute-done((f32[5,8,128]{2,1,0:T(8,128)S(1)}, f32[5,8,128]{2,1,0:T(8,128)S(1)}, u32[]{:S(2)}, u32[]{:S(2)}) %collective-permute-start.9) | collective-permute-done | bytes 20512 | tf_op jit(solution)/shard_map/ppermute | solution.py:35
  30.5 6.0 %collective-permute-start.10 = (f32[5,8,128]{2,1,0:T(8,128)S(1)}, f32[5,8,128]{2,1,0:T(8,128)S(1)}, u32[]{:S(2)}, u32[]{:S(2)}) collective-permute-start(f32[5,8,128]{2,1,0:T(8,128)S(1)} %shard_map.91.refs_0_), channel_id=1, source_target_pairs={{0,1},{1,0},{2,3},{3,2},{4,5},{5,4},{6,7},{7,6},{8,9},{9,8},{10,11... | collective-permute-start | bytes 61448 | tf_op jit(solution)/shard_map/ppermute | solution.py:39
  37.4 1.4 %shard_map.92 = (f32[8,640]{1,0:T(8,128)S(1)}, f32[23,8,128]{2,1,0:T(8,128)S(1)}) custom-call(f32[5,8,128]{2,1,0:T(8,128)S(1)} %shard_map.91.refs_0_, f32[5,8,128]{2,1,0:T(8,128)S(1)} %collective-permute-done.10.refs_1_, bf16[640,5760]{1,0:T(8,128)(2,1)S(1)} %get-tuple-element.32.refs_2_.refs_1_), custom_call_target="tpu_custom_call" | custom-call | tf_op jit(solution)/shard_map/pallas_call | solution.py:73
  40.1 2.6 %collective-permute-start.13 = (f32[23,8,128]{2,1,0:T(8,128)S(1)}, f32[23,8,128]{2,1,0:T(8,128)S(1)}, u32[]{:S(2)}, u32[]{:S(2)}) collective-permute-start(f32[23,8,128]{2,1,0:T(8,128)S(1)} %shard_map.95.refs_2_.rest_0_.refs_0_), channel_id=1, source_target_pairs={{0,6},{1,97},{2,4},{3,99},{4,2},{5,101},{6,0},{7,103},{8,14},{9,10... | collective-permute-start | bytes 282632 | tf_op jit(solution)/shard_map/ppermute | solution.py:35
  43.2 1.4 %shard_map.97 = (bf16[1,640,5760]{2,1,0:T(8,128)(2,1)}, f32[1,8,128]{2,1,0:T(8,128)S(1)}) custom-call(bf16[48,640]{1,0:T(8,128)(2,1)S(1)} %get-tuple-element.35.refs_2_.l_ref, bf16[48,5760]{1,0:T(8,128)(2,1)S(1)} %get-tuple-element.36.r_ref, bf16[640,5760]{1,0:T(8,128)(2,1)S(1)} %get-tuple-element.37.g_ref, bf16[640,5760]{1,0:T(8,128)(2,1)S(1)} %get-tuple-element.38.e_ref, ...), custom_call_target="tpu_custom_call" | custom-call | flops 10000000000 | tf_op jit(solution)/shard_map/pallas_call | solution.py:245
  45.1 2.6 %collective-permute-start.14 = (f32[23,8,128]{2,1,0:T(8,128)S(1)}, f32[23,8,128]{2,1,0:T(8,128)S(1)}, u32[]{:S(2)}, u32[]{:S(2)}) collective-permute-start(f32[23,8,128]{2,1,0:T(8,128)S(1)} %shard_map.98.refs_2_.refs_0_), channel_id=1, source_target_pairs={{0,24},{1,7},{2,26},{3,5},{4,28},{5,3},{6,30},{7,1},{8,16},{9,15},... | collective-permute-start | bytes 282632 | tf_op jit(solution)/shard_map/ppermute | solution.py:35
  48.1 2.3 %collective-permute-start.18 = (f32[32,8,128]{2,1,0:T(8,128)S(1)}, f32[32,8,128]{2,1,0:T(8,128)S(1)}, u32[]{:S(2)}, u32[]{:S(2)}) collective-permute-start(f32[32,8,128]{2,1,0:T(8,128)S(1)} %shard_map.99.refs_1_.rest_2_.refs_0_), channel_id=1, source_target_pairs={{0,24},{1,7},{2,26},{3,5},{4,28},{5,3},{6,30},{7,1},{8,16},{9,15},... | collective-permute-start | bytes 393224 | tf_op jit(solution)/shard_map/ppermute | solution.py:35
  50.7 2.6 %shard_map.102 = (bf16[1,640,5760]{2,1,0:T(8,128)(2,1)}, f32[1,8,128]{2,1,0:T(8,128)S(1)}) custom-call(bf16[48,640]{1,0:T(8,128)(2,1)S(1)} %get-tuple-element.35.refs_2_.l_ref, bf16[48,5760]{1,0:T(8,128)(2,1)S(1)} %get-tuple-element.36.r_ref, bf16[640,5760]{1,0:T(8,128)(2,1)S(1)} %get-tuple-element.37.g_ref, ...), custom_call_target="tpu_custom_call", output_to_operand_aliasing={{0}: (4, {})} | custom-call | flops 10000000000 | tf_op jit(solution)/shard_map/pallas_call | solution.py:245
  53.3 1.1 %collective-permute-done.16.refs_1_ = f32[23,8,128]{2,1,0:T(8,128)S(1)} collective-permute-done((f32[23,8,128]{2,1,0:T(8,128)S(1)}, f32[23,8,128]{2,1,0:T(8,128)S(1)}, u32[]{:S(2)}, u32[]{:S(2)}) %collective-permute-start.16) | collective-permute-done | bytes 94240 | tf_op jit(solution)/shard_map/ppermute | solution.py:35
  56.1 2.0 %collective-permute-done.17.refs_1_ = f32[23,8,128]{2,1,0:T(8,128)S(1)} collective-permute-done((f32[23,8,128]{2,1,0:T(8,128)S(1)}, f32[23,8,128]{2,1,0:T(8,128)S(1)}, u32[]{:S(2)}, u32[]{:S(2)}) %collective-permute-start.17) | collective-permute-done | bytes 94240 | tf_op jit(solution)/shard_map/ppermute | solution.py:35
  58.2 1.3 %collective-permute-done.20.refs_1_ = f32[32,8,128]{2,1,0:T(8,128)S(1)} collective-permute-done((f32[32,8,128]{2,1,0:T(8,128)S(1)}, f32[32,8,128]{2,1,0:T(8,128)S(1)}, u32[]{:S(2)}, u32[]{:S(2)}) %collective-permute-start.20) | collective-permute-done | bytes 131104 | tf_op jit(solution)/shard_map/ppermute | solution.py:35
  59.8 2.5 %collective-permute-done.19.refs_1_ = f32[23,8,128]{2,1,0:T(8,128)S(1)} collective-permute-done((f32[23,8,128]{2,1,0:T(8,128)S(1)}, f32[23,8,128]{2,1,0:T(8,128)S(1)}, u32[]{:S(2)}, u32[]{:S(2)}) %collective-permute-start.19) | collective-permute-done | bytes 94240 | tf_op jit(solution)/shard_map/ppermute | solution.py:35
  62.3 3.4 %collective-permute-start.21 = (f32[23,8,128]{2,1,0:T(8,128)S(1)}, f32[23,8,128]{2,1,0:T(8,128)S(1)}, u32[]{:S(2)}, u32[]{:S(2)}) collective-permute-start(f32[23,8,128]{2,1,0:T(8,128)S(1)} %shard_map.109.rest_1_.refs_0_), channel_id=1, source_target_pairs={{0,96},{1,25},{2,98},{3,27},{4,100},{5,29},{6,102},{7,31},{8,104},... | collective-permute-start | bytes 282632 | tf_op jit(solution)/shard_map/ppermute | solution.py:35
  65.7 1.4 %shard_map.110 = (bf16[1,640,5760]{2,1,0:T(8,128)(2,1)}, f32[1,8,128]{2,1,0:T(8,128)S(1)}) custom-call(bf16[48,640]{1,0:T(8,128)(2,1)S(1)} %get-tuple-element.35.refs_2_.l_ref, bf16[48,5760]{1,0:T(8,128)(2,1)S(1)} %get-tuple-element.36.r_ref, bf16[640,5760]{1,0:T(8,128)(2,1)S(1)} %get-tuple-element.37.g_ref, ...), custom_call_target="tpu_custom_call", output_to_operand_aliasing={{0}: (4, {})} | custom-call | flops 10000000000 | tf_op jit(solution)/shard_map/pallas_call | solution.py:245
  67.2 6.4 %collective-permute-start.24 = (f32[125,8,128]{2,1,0:T(8,128)S(1)}, f32[125,8,128]{2,1,0:T(8,128)S(1)}, u32[]{:S(2)}, u32[]{:S(2)}) collective-permute-start(f32[125,8,128]{2,1,0:T(8,128)S(1)} %shard_map.111.refs_1_.refs_0_), channel_id=1, source_target_pairs={{0,1},{1,0},{2,3},{3,2},{4,5},{5,4},{6,7},{7,6},{8,9},{9,8},{10,11... | collective-permute-start | bytes 1536008 | tf_op jit(solution)/shard_map/ppermute | solution.py:39
  (69 shorter events, 14.1 us)
Async XLA Ops:
  0.6 9.7 %collective-permute-start.1 = (f32[200,1280]{1,0:T(8,128)}, f32[200,1280]{1,0:T(8,128)S(1)}, u32[]{:S(2)}, u32[]{:S(2)}) collective-permute-start(f32[200,1280]{1,0:T(8,128)} %refs_0_.1), channel_id=1, source_target_pairs={{0,1},{1,0},{2,3},{3,2},{4,5},{5,4},{6,7},{7,6},{8,9},{9,8},{10,11... | collective-permute-start | bytes 3072008 | tf_op jit(solution)/shard_map/ppermute | solution.py:39
  8.8 2.7 %collective-permute-start = (f32[5,8,128]{2,1,0:T(8,128)S(1)}, f32[5,8,128]{2,1,0:T(8,128)S(1)}, u32[]{:S(2)}, u32[]{:S(2)}) collective-permute-start(f32[5,8,128]{2,1,0:T(8,128)S(1)} %get-tuple-element.27.refs_2_.refs_0_), channel_id=1, source_target_pairs={{0,2},{1,33},{2,0},{3,35},{4,6},{5,37},{6,4},{7,39},{8,10},{9,41},... | collective-permute-start | bytes 61448 | tf_op jit(solution)/shard_map/ppermute | solution.py:35
  10.4 6.8 %collective-permute-start.4 = (f32[63,8,128]{2,1,0:T(8,128)S(1)}, f32[63,8,128]{2,1,0:T(8,128)S(1)}, u32[]{:S(2)}, u32[]{:S(2)}) collective-permute-start(f32[63,8,128]{2,1,0:T(8,128)S(1)} %get-tuple-element.28.refs_0_), channel_id=1, source_target_pairs={{0,2},{1,33},{2,0},{3,35},{4,6},{5,37},{6,4},{7,39},{8,10},{9,41},... | collective-permute-start | bytes 774152 | tf_op jit(solution)/shard_map/ppermute | solution.py:35
  11.6 4.0 %collective-permute-start.2 = (f32[5,8,128]{2,1,0:T(8,128)S(1)}, f32[5,8,128]{2,1,0:T(8,128)S(1)}, u32[]{:S(2)}, u32[]{:S(2)}) collective-permute-start(f32[5,8,128]{2,1,0:T(8,128)S(1)} %shard_map.78.refs_0_), channel_id=1, source_target_pairs={{0,6},{1,97},{2,4},{3,99},{4,2},{5,101},{6,0},{7,103},{8,14},{9,10... | collective-permute-start | bytes 61448 | tf_op jit(solution)/shard_map/ppermute | solution.py:35
  15.6 2.8 %collective-permute-start.3 = (f32[5,8,128]{2,1,0:T(8,128)S(1)}, f32[5,8,128]{2,1,0:T(8,128)S(1)}, u32[]{:S(2)}, u32[]{:S(2)}) collective-permute-start(f32[5,8,128]{2,1,0:T(8,128)S(1)} %shard_map.79.refs_2_.refs_0_), channel_id=1, source_target_pairs={{0,32},{1,9},{2,34},{3,11},{4,36},{5,13},{6,38},{7,15},{8,40},{9,1... | collective-permute-start | bytes 61448 | tf_op jit(solution)/shard_map/ppermute | solution.py:35
  17.2 4.7 %collective-permute-start.6 = (f32[32,8,128]{2,1,0:T(8,128)S(1)}, f32[32,8,128]{2,1,0:T(8,128)S(1)}, u32[]{:S(2)}, u32[]{:S(2)}) collective-permute-start(f32[32,8,128]{2,1,0:T(8,128)S(1)} %get-tuple-element.30.refs_0_), channel_id=1, source_target_pairs={{0,32},{1,9},{2,34},{3,11},{4,36},{5,13},{6,38},{7,15},{8,40},{9,1... | collective-permute-start | bytes 393224 | tf_op jit(solution)/shard_map/ppermute | solution.py:35
  18.4 5.4 %collective-permute-start.5 = (f32[5,8,128]{2,1,0:T(8,128)S(1)}, f32[5,8,128]{2,1,0:T(8,128)S(1)}, u32[]{:S(2)}, u32[]{:S(2)}) collective-permute-start(f32[5,8,128]{2,1,0:T(8,128)S(1)} %shard_map.82.refs_2_.refs_0_), channel_id=1, source_target_pairs={{0,96},{1,25},{2,98},{3,27},{4,100},{5,29},{6,102},{7,31},{8,104},... | collective-permute-start | bytes 61448 | tf_op jit(solution)/shard_map/ppermute | solution.py:35
  22.0 5.1 %collective-permute-start.8 = (f32[32,8,128]{2,1,0:T(8,128)S(1)}, f32[32,8,128]{2,1,0:T(8,128)S(1)}, u32[]{:S(2)}, u32[]{:S(2)}) collective-permute-start(f32[32,8,128]{2,1,0:T(8,128)S(1)} %shard_map.83.refs_0_), channel_id=1, source_target_pairs={{0,96},{1,25},{2,98},{3,27},{4,100},{5,29},{6,102},{7,31},{8,104},... | collective-permute-start | bytes 393224 | tf_op jit(solution)/shard_map/ppermute | solution.py:35
  23.8 3.9 %collective-permute-start.7 = (f32[5,8,128]{2,1,0:T(8,128)S(1)}, f32[5,8,128]{2,1,0:T(8,128)S(1)}, u32[]{:S(2)}, u32[]{:S(2)}) collective-permute-start(f32[5,8,128]{2,1,0:T(8,128)S(1)} %shard_map.85.refs_2_.refs_0_), channel_id=1, source_target_pairs={{0,24},{1,7},{2,26},{3,5},{4,28},{5,3},{6,30},{7,1},{8,16},{9,15},... | collective-permute-start | bytes 61448 | tf_op jit(solution)/shard_map/ppermute | solution.py:35
  27.7 2.8 %collective-permute-start.9 = (f32[5,8,128]{2,1,0:T(8,128)S(1)}, f32[5,8,128]{2,1,0:T(8,128)S(1)}, u32[]{:S(2)}, u32[]{:S(2)}) collective-permute-start(f32[5,8,128]{2,1,0:T(8,128)S(1)} %shard_map.88.refs_1_.refs_0_), channel_id=1, source_target_pairs={{0,8},{1,3},{2,10},{3,1},{4,12},{5,7},{6,14},{7,5},{8,0},{9,11},{1... | collective-permute-start | bytes 61448 | tf_op jit(solution)/shard_map/ppermute | solution.py:35
  30.5 6.9 %collective-permute-start.10 = (f32[5,8,128]{2,1,0:T(8,128)S(1)}, f32[5,8,128]{2,1,0:T(8,128)S(1)}, u32[]{:S(2)}, u32[]{:S(2)}) collective-permute-start(f32[5,8,128]{2,1,0:T(8,128)S(1)} %shard_map.91.refs_0_), channel_id=1, source_target_pairs={{0,1},{1,0},{2,3},{3,2},{4,5},{5,4},{6,7},{7,6},{8,9},{9,8},{10,11... | collective-permute-start | bytes 61448 | tf_op jit(solution)/shard_map/ppermute | solution.py:39
  36.5 6.1 %collective-permute-start.12 = (f32[32,8,128]{2,1,0:T(8,128)S(1)}, f32[32,8,128]{2,1,0:T(8,128)S(1)}, u32[]{:S(2)}, u32[]{:S(2)}) collective-permute-start(f32[32,8,128]{2,1,0:T(8,128)S(1)} %shard_map.89.refs_0_), channel_id=1, source_target_pairs={{0,8},{1,3},{2,10},{3,1},{4,12},{5,7},{6,14},{7,5},{8,0},{9,11},{1... | collective-permute-start | bytes 393224 | tf_op jit(solution)/shard_map/ppermute | solution.py:35
  40.1 5.0 %collective-permute-start.13 = (f32[23,8,128]{2,1,0:T(8,128)S(1)}, f32[23,8,128]{2,1,0:T(8,128)S(1)}, u32[]{:S(2)}, u32[]{:S(2)}) collective-permute-start(f32[23,8,128]{2,1,0:T(8,128)S(1)} %shard_map.95.refs_2_.rest_0_.refs_0_), channel_id=1, source_target_pairs={{0,6},{1,97},{2,4},{3,99},{4,2},{5,101},{6,0},{7,103},{8,14},{9,10... | collective-permute-start | bytes 282632 | tf_op jit(solution)/shard_map/ppermute | solution.py:35
  42.7 5.4 %collective-permute-start.15 = (f32[32,8,128]{2,1,0:T(8,128)S(1)}, f32[32,8,128]{2,1,0:T(8,128)S(1)}, u32[]{:S(2)}, u32[]{:S(2)}) collective-permute-start(f32[32,8,128]{2,1,0:T(8,128)S(1)} %shard_map.96.rest_1_.refs_0_), channel_id=1, source_target_pairs={{0,6},{1,97},{2,4},{3,99},{4,2},{5,101},{6,0},{7,103},{8,14},{9,10... | collective-permute-start | bytes 393224 | tf_op jit(solution)/shard_map/ppermute | solution.py:35
  45.1 5.3 %collective-permute-start.14 = (f32[23,8,128]{2,1,0:T(8,128)S(1)}, f32[23,8,128]{2,1,0:T(8,128)S(1)}, u32[]{:S(2)}, u32[]{:S(2)}) collective-permute-start(f32[23,8,128]{2,1,0:T(8,128)S(1)} %shard_map.98.refs_2_.refs_0_), channel_id=1, source_target_pairs={{0,24},{1,7},{2,26},{3,5},{4,28},{5,3},{6,30},{7,1},{8,16},{9,15},... | collective-permute-start | bytes 282632 | tf_op jit(solution)/shard_map/ppermute | solution.py:35
  48.1 7.0 %collective-permute-start.18 = (f32[32,8,128]{2,1,0:T(8,128)S(1)}, f32[32,8,128]{2,1,0:T(8,128)S(1)}, u32[]{:S(2)}, u32[]{:S(2)}) collective-permute-start(f32[32,8,128]{2,1,0:T(8,128)S(1)} %shard_map.99.refs_1_.rest_2_.refs_0_), channel_id=1, source_target_pairs={{0,24},{1,7},{2,26},{3,5},{4,28},{5,3},{6,30},{7,1},{8,16},{9,15},... | collective-permute-start | bytes 393224 | tf_op jit(solution)/shard_map/ppermute | solution.py:35
  50.4 4.0 %collective-permute-start.16 = (f32[23,8,128]{2,1,0:T(8,128)S(1)}, f32[23,8,128]{2,1,0:T(8,128)S(1)}, u32[]{:S(2)}, u32[]{:S(2)}) collective-permute-start(f32[23,8,128]{2,1,0:T(8,128)S(1)} %shard_map.101.rest_1_.refs_0_), channel_id=1, source_target_pairs={{0,8},{1,3},{2,10},{3,1},{4,12},{5,7},{6,14},{7,5},{8,0},{9,11},{1... | collective-permute-start | bytes 282632 | tf_op jit(solution)/shard_map/ppermute | solution.py:35
  54.4 3.7 %collective-permute-start.17 = (f32[23,8,128]{2,1,0:T(8,128)S(1)}, f32[23,8,128]{2,1,0:T(8,128)S(1)}, u32[]{:S(2)}, u32[]{:S(2)}) collective-permute-start(f32[23,8,128]{2,1,0:T(8,128)S(1)} %shard_map.103.refs_2_.refs_0_), channel_id=1, source_target_pairs={{0,32},{1,9},{2,34},{3,11},{4,36},{5,13},{6,38},{7,15},{8,40},{9,1... | collective-permute-start | bytes 282632 | tf_op jit(solution)/shard_map/ppermute | solution.py:35
  55.1 4.4 %collective-permute-start.20 = (f32[32,8,128]{2,1,0:T(8,128)S(1)}, f32[32,8,128]{2,1,0:T(8,128)S(1)}, u32[]{:S(2)}, u32[]{:S(2)}) collective-permute-start(f32[32,8,128]{2,1,0:T(8,128)S(1)} %shard_map.104.refs_1_.refs_0_), channel_id=1, source_target_pairs={{0,32},{1,9},{2,34},{3,11},{4,36},{5,13},{6,38},{7,15},{8,40},{9,1... | collective-permute-start | bytes 393224 | tf_op jit(solution)/shard_map/ppermute | solution.py:35
  58.1 4.2 %collective-permute-start.19 = (f32[23,8,128]{2,1,0:T(8,128)S(1)}, f32[23,8,128]{2,1,0:T(8,128)S(1)}, u32[]{:S(2)}, u32[]{:S(2)}) collective-permute-start(f32[23,8,128]{2,1,0:T(8,128)S(1)} %shard_map.106.refs_2_.refs_0_), channel_id=1, source_target_pairs={{0,2},{1,33},{2,0},{3,35},{4,6},{5,37},{6,4},{7,39},{8,10},{9,41},... | collective-permute-start | bytes 282632 | tf_op jit(solution)/shard_map/ppermute | solution.py:35
  59.6 7.6 %collective-permute-start.22 = (f32[63,8,128]{2,1,0:T(8,128)S(1)}, f32[63,8,128]{2,1,0:T(8,128)S(1)}, u32[]{:S(2)}, u32[]{:S(2)}) collective-permute-start(f32[63,8,128]{2,1,0:T(8,128)S(1)} %shard_map.107.refs_1_.refs_0_), channel_id=1, source_target_pairs={{0,2},{1,33},{2,0},{3,35},{4,6},{5,37},{6,4},{7,39},{8,10},{9,41},... | collective-permute-start | bytes 774152 | tf_op jit(solution)/shard_map/ppermute | solution.py:35
  62.3 11.3 %collective-permute-start.21 = (f32[23,8,128]{2,1,0:T(8,128)S(1)}, f32[23,8,128]{2,1,0:T(8,128)S(1)}, u32[]{:S(2)}, u32[]{:S(2)}) collective-permute-start(f32[23,8,128]{2,1,0:T(8,128)S(1)} %shard_map.109.rest_1_.refs_0_), channel_id=1, source_target_pairs={{0,96},{1,25},{2,98},{3,27},{4,100},{5,29},{6,102},{7,31},{8,104},... | collective-permute-start | bytes 282632 | tf_op jit(solution)/shard_map/ppermute | solution.py:35
  67.2 7.9 %collective-permute-start.24 = (f32[125,8,128]{2,1,0:T(8,128)S(1)}, f32[125,8,128]{2,1,0:T(8,128)S(1)}, u32[]{:S(2)}, u32[]{:S(2)}) collective-permute-start(f32[125,8,128]{2,1,0:T(8,128)S(1)} %shard_map.111.refs_1_.refs_0_), channel_id=1, source_target_pairs={{0,1},{1,0},{2,3},{3,2},{4,5},{5,4},{6,7},{7,6},{8,9},{9,8},{10,11... | collective-permute-start | bytes 1536008 | tf_op jit(solution)/shard_map/ppermute | solution.py:39
  73.6 2.5 %collective-permute-start.23 = (f32[23,8,128]{2,1,0:T(8,128)S(1)}, f32[23,8,128]{2,1,0:T(8,128)S(1)}, u32[]{:S(2)}, u32[]{:S(2)}) collective-permute-start(f32[23,8,128]{2,1,0:T(8,128)S(1)} %shard_map.113.refs_2_.refs_0_), channel_id=1, source_target_pairs={{0,1},{1,0},{2,3},{3,2},{4,5},{5,4},{6,7},{7,6},{8,9},{9,8},{10,11... | collective-permute-start | bytes 282632 | tf_op jit(solution)/shard_map/ppermute | solution.py:39
  (2 other events, 9.5 us)

commit v3 on v2

--- a/solution.py
+++ b/solution.py
@@ -14,9 +14,9 @@
 RING_BIT = {"x": 1, "z": 3, "y": 5}
 AROUND = ("x", "y", "z")
 P_HOPS = (("x0", "x1", "y0", "y1", "z1", "z0"), ("y0", "y1", "z0", "z1", "x1", "x0"))
-Q_HOPS = (("x1", "z1", "z0", "y0", "x0", "y1"), ("y1", "x1", "x0", "z0", "y0", "z1"))
+Q_HOPS = (("x1", "z1", "y0", "z0", "x0", "y1"), ("y1", "x1", "z0", "x0", "y0", "z1"))
 HALVINGS = (0, 2)
-SLABS = (1, 0, 3, 0, 0, 1)
+SLABS = (1, 0, 0, 3, 0, 1)
 LAST_PARTS = 3
 SHORT = pl.CostEstimate(flops=0, bytes_accessed=0, transcendentals=0)
 LONG = pl.CostEstimate(flops=10_000_000_000, bytes_accessed=0, transcendentals=0)
@@ -427,11 +427,11 @@
         if step == steps - 1:
             fresh, done = residual_rows(sum(SLABS[:step]), SLABS[step], left, right, g_here, r_here, fresh, after)
             after = [done]
-        if step in (0, 1, 3):
+        if step < 3:
             v_keep = add(v_keep, v_got, after, LONG)
         elif step > 3:
             v_keep = join(steps - 1 - step, sizes[steps - 1 - step], v_keep, v_got, after)
-        if step != 2:
+        if step != 3:
             v_got = swap(v_keep, Q_HOPS, step) if step < steps - 1 else swap_cores(v_keep)
         if SLABS[step] and step < steps - 1:
             fresh, done = residual_rows(

time: 77.2 us -> 75.2 us (0.974)
  waiting for transfers between devices: 15.4 us -> 13.3 us
    ppermute x20, waiting for transfers between devices: 14 us -> 12.4 us  [swap(): lax.ppermute(x, AXES, [(i, partner(i, pair)) for i in range(lax.axis_size...]
  transfers between devices with their start and end apart: 25 -> 25, of which waited for: 15 -> 14; matrix products, arithmetic and copies ran while one was open for 0% -> 0% of each run, Pallas kernels for 21% -> 21%
where the time goes in v3:
time: 75.2 us; the launch traced here: 75.1 us
  starting transfers between devices  44.1 us (59%)
  Pallas kernels  16.9 us (22%)
  waiting for transfers between devices  13.3 us (18%)
  between operations  0.8 us (1%)
    ppermute x20, starting transfers between devices, swap(): lax.ppermute(x, AXES, [(i, partner(i, pair)) for i in range(lax.axis_size...  29.4 us
    ppermute x5, starting transfers between devices, swap_cores(): lax.ppermute(x, AXES, [(i, i ^ 1) for i in range(lax.axis_size(AXES))])  14.7 us
    ppermute x20, waiting for transfers between devices, swap(): lax.ppermute(x, AXES, [(i, partner(i, pair)) for i in range(lax.axis_size...  12.4 us
    pallas_call x1, Pallas kernels, left_product(): pl.pallas_call(body, in_specs=[pl.BlockSpec(memory_space=pltpu.HBM)] * 3,...  6.7 us
    pallas_call x3, Pallas kernels, residual_rows(): pl.pallas_call(body, in_specs=[vmem] * 4 + [anywhere] * len(others), out_...  5.47 us
    pallas_call x37, Pallas kernels, call(): pl.pallas_call(kernel, in_specs=[pl.BlockSpec(memory_space=pltpu.VMEM)] *...  4.7 us
  transfers between devices with their start and end apart: 25, of which 14 were waited for; matrix products, arithmetic and copies ran while one was open for 0% of the time, Pallas kernels for 21%

profile of v3, /device:TPU:1, one launch (start us, length us, event | category | flops | bytes accessed | tf_op | source)
XLA Modules:
  0.0 75.1 jit_solution(13322313761764002013)
XLA Ops:
  0.6 1.5 %collective-permute-start.1 = (f32[200,1280]{1,0:T(8,128)}, f32[200,1280]{1,0:T(8,128)S(1)}, u32[]{:S(2)}, u32[]{:S(2)}) collective-permute-start(f32[200,1280]{1,0:T(8,128)} %refs_0_.1), channel_id=1, source_target_pairs={{0,1},{1,0},{2,3},{3,2},{4,5},{5,4},{6,7},{7,6},{8,9},{9,8},{10,11... | collective-permute-start | bytes 3072008 | tf_op jit(solution)/shard_map/ppermute | solution.py:39
  2.1 6.7 %shard_map.75 = (f32[5,8,128]{2,1,0:T(8,128)S(1)}, bf16[640,5760]{1,0:T(8,128)(2,1)S(1)}, bf16[640,5760]{1,0:T(8,128)(2,1)S(1)}, bf16[640,5760]{1,0:T(8,128)(2,1)S(1)}) custom-call(bf16[1,640,5760]{2,1,0:T(8,128)(2,1)} %g_hbm.1, bf16[1,640,5760]{2,1,0:T(8,128)(2,1)} %r_hbm.1, f32[8,5760]{1,0:T(8,128)} %bitcast.2), custom_call_target="tpu_custom_call" | custom-call | tf_op jit(solution)/shard_map/pallas_call | solution.py:116
  8.8 1.5 %collective-permute-start = (f32[5,8,128]{2,1,0:T(8,128)S(1)}, f32[5,8,128]{2,1,0:T(8,128)S(1)}, u32[]{:S(2)}, u32[]{:S(2)}) collective-permute-start(f32[5,8,128]{2,1,0:T(8,128)S(1)} %get-tuple-element.27.refs_2_.refs_0_), channel_id=1, source_target_pairs={{0,2},{1,33},{2,0},{3,35},{4,6},{5,37},{6,4},{7,39},{8,10},{9,41},... | collective-permute-start | bytes 61448 | tf_op jit(solution)/shard_map/ppermute | solution.py:35
  11.6 2.8 %collective-permute-start.2 = (f32[5,8,128]{2,1,0:T(8,128)S(1)}, f32[5,8,128]{2,1,0:T(8,128)S(1)}, u32[]{:S(2)}, u32[]{:S(2)}) collective-permute-start(f32[5,8,128]{2,1,0:T(8,128)S(1)} %shard_map.78.refs_0_), channel_id=1, source_target_pairs={{0,6},{1,97},{2,4},{3,99},{4,2},{5,101},{6,0},{7,103},{8,14},{9,10... | collective-permute-start | bytes 61448 | tf_op jit(solution)/shard_map/ppermute | solution.py:35
  14.4 1.2 %collective-permute-done.2.refs_1_ = f32[5,8,128]{2,1,0:T(8,128)S(1)} collective-permute-done((f32[5,8,128]{2,1,0:T(8,128)S(1)}, f32[5,8,128]{2,1,0:T(8,128)S(1)}, u32[]{:S(2)}, u32[]{:S(2)}) %collective-permute-start.2) | collective-permute-done | bytes 20512 | tf_op jit(solution)/shard_map/ppermute | solution.py:35
  15.6 1.6 %collective-permute-start.3 = (f32[5,8,128]{2,1,0:T(8,128)S(1)}, f32[5,8,128]{2,1,0:T(8,128)S(1)}, u32[]{:S(2)}, u32[]{:S(2)}) collective-permute-start(f32[5,8,128]{2,1,0:T(8,128)S(1)} %shard_map.79.refs_2_.refs_0_), channel_id=1, source_target_pairs={{0,32},{1,9},{2,34},{3,11},{4,36},{5,13},{6,38},{7,15},{8,40},{9,1... | collective-permute-start | bytes 61448 | tf_op jit(solution)/shard_map/ppermute | solution.py:35
  18.4 3.6 %collective-permute-start.5 = (f32[5,8,128]{2,1,0:T(8,128)S(1)}, f32[5,8,128]{2,1,0:T(8,128)S(1)}, u32[]{:S(2)}, u32[]{:S(2)}) collective-permute-start(f32[5,8,128]{2,1,0:T(8,128)S(1)} %shard_map.82.refs_2_.refs_0_), channel_id=1, source_target_pairs={{0,96},{1,25},{2,98},{3,27},{4,100},{5,29},{6,102},{7,31},{8,104},... | collective-permute-start | bytes 61448 | tf_op jit(solution)/shard_map/ppermute | solution.py:35
  22.0 1.8 %collective-permute-start.8 = (f32[32,8,128]{2,1,0:T(8,128)S(1)}, f32[32,8,128]{2,1,0:T(8,128)S(1)}, u32[]{:S(2)}, u32[]{:S(2)}) collective-permute-start(f32[32,8,128]{2,1,0:T(8,128)S(1)} %shard_map.83.refs_0_), channel_id=1, source_target_pairs={{0,96},{1,25},{2,98},{3,27},{4,100},{5,29},{6,102},{7,31},{8,104},... | collective-permute-start | bytes 393224 | tf_op jit(solution)/shard_map/ppermute | solution.py:35
  23.8 2.6 %collective-permute-start.7 = (f32[5,8,128]{2,1,0:T(8,128)S(1)}, f32[5,8,128]{2,1,0:T(8,128)S(1)}, u32[]{:S(2)}, u32[]{:S(2)}) collective-permute-start(f32[5,8,128]{2,1,0:T(8,128)S(1)} %shard_map.85.refs_2_.refs_0_), channel_id=1, source_target_pairs={{0,24},{1,7},{2,26},{3,5},{4,28},{5,3},{6,30},{7,1},{8,16},{9,15},... | collective-permute-start | bytes 61448 | tf_op jit(solution)/shard_map/ppermute | solution.py:35
  28.5 2.1 %collective-permute-done.9.refs_1_ = f32[5,8,128]{2,1,0:T(8,128)S(1)} collective-permute-done((f32[5,8,128]{2,1,0:T(8,128)S(1)}, f32[5,8,128]{2,1,0:T(8,128)S(1)}, u32[]{:S(2)}, u32[]{:S(2)}) %collective-permute-start.9) | collective-permute-done | bytes 20512 | tf_op jit(solution)/shard_map/ppermute | solution.py:35
  30.5 6.0 %collective-permute-start.10 = (f32[5,8,128]{2,1,0:T(8,128)S(1)}, f32[5,8,128]{2,1,0:T(8,128)S(1)}, u32[]{:S(2)}, u32[]{:S(2)}) collective-permute-start(f32[5,8,128]{2,1,0:T(8,128)S(1)} %shard_map.91.refs_0_), channel_id=1, source_target_pairs={{0,1},{1,0},{2,3},{3,2},{4,5},{5,4},{6,7},{7,6},{8,9},{9,8},{10,11... | collective-permute-start | bytes 61448 | tf_op jit(solution)/shard_map/ppermute | solution.py:39
  37.4 1.4 %shard_map.92 = (f32[8,640]{1,0:T(8,128)S(1)}, f32[23,8,128]{2,1,0:T(8,128)S(1)}) custom-call(f32[5,8,128]{2,1,0:T(8,128)S(1)} %shard_map.91.refs_0_, f32[5,8,128]{2,1,0:T(8,128)S(1)} %collective-permute-done.10.refs_1_, bf16[640,5760]{1,0:T(8,128)(2,1)S(1)} %get-tuple-element.32.refs_2_.refs_1_), custom_call_target="tpu_custom_call" | custom-call | tf_op jit(solution)/shard_map/pallas_call | solution.py:73
  40.1 2.6 %collective-permute-start.13 = (f32[23,8,128]{2,1,0:T(8,128)S(1)}, f32[23,8,128]{2,1,0:T(8,128)S(1)}, u32[]{:S(2)}, u32[]{:S(2)}) collective-permute-start(f32[23,8,128]{2,1,0:T(8,128)S(1)} %shard_map.95.refs_2_.rest_0_.refs_0_), channel_id=1, source_target_pairs={{0,6},{1,97},{2,4},{3,99},{4,2},{5,101},{6,0},{7,103},{8,14},{9,10... | collective-permute-start | bytes 282632 | tf_op jit(solution)/shard_map/ppermute | solution.py:35
  43.2 1.4 %shard_map.97 = (bf16[1,640,5760]{2,1,0:T(8,128)(2,1)}, f32[1,8,128]{2,1,0:T(8,128)S(1)}) custom-call(bf16[48,640]{1,0:T(8,128)(2,1)S(1)} %get-tuple-element.35.refs_2_.l_ref, bf16[48,5760]{1,0:T(8,128)(2,1)S(1)} %get-tuple-element.36.r_ref, bf16[640,5760]{1,0:T(8,128)(2,1)S(1)} %get-tuple-element.37.g_ref, bf16[640,5760]{1,0:T(8,128)(2,1)S(1)} %get-tuple-element.38.e_ref, ...), custom_call_target="tpu_custom_call" | custom-call | flops 10000000000 | tf_op jit(solution)/shard_map/pallas_call | solution.py:245
  45.1 2.6 %collective-permute-start.14 = (f32[23,8,128]{2,1,0:T(8,128)S(1)}, f32[23,8,128]{2,1,0:T(8,128)S(1)}, u32[]{:S(2)}, u32[]{:S(2)}) collective-permute-start(f32[23,8,128]{2,1,0:T(8,128)S(1)} %shard_map.98.refs_2_.refs_0_), channel_id=1, source_target_pairs={{0,24},{1,7},{2,26},{3,5},{4,28},{5,3},{6,30},{7,1},{8,16},{9,15},... | collective-permute-start | bytes 282632 | tf_op jit(solution)/shard_map/ppermute | solution.py:35
  48.1 2.3 %collective-permute-start.17 = (f32[32,8,128]{2,1,0:T(8,128)S(1)}, f32[32,8,128]{2,1,0:T(8,128)S(1)}, u32[]{:S(2)}, u32[]{:S(2)}) collective-permute-start(f32[32,8,128]{2,1,0:T(8,128)S(1)} %shard_map.99.refs_1_.refs_0_), channel_id=1, source_target_pairs={{0,24},{1,7},{2,26},{3,5},{4,28},{5,3},{6,30},{7,1},{8,16},{9,15},... | collective-permute-start | bytes 393224 | tf_op jit(solution)/shard_map/ppermute | solution.py:35
  51.1 2.1 %collective-permute-done.17.refs_1_ = f32[32,8,128]{2,1,0:T(8,128)S(1)} collective-permute-done((f32[32,8,128]{2,1,0:T(8,128)S(1)}, f32[32,8,128]{2,1,0:T(8,128)S(1)}, u32[]{:S(2)}, u32[]{:S(2)}) %collective-permute-start.17) | collective-permute-done | bytes 131104 | tf_op jit(solution)/shard_map/ppermute | solution.py:35
  54.5 2.6 %shard_map.105 = (bf16[1,640,5760]{2,1,0:T(8,128)(2,1)}, f32[1,8,128]{2,1,0:T(8,128)S(1)}) custom-call(bf16[48,640]{1,0:T(8,128)(2,1)S(1)} %get-tuple-element.35.refs_2_.l_ref, bf16[48,5760]{1,0:T(8,128)(2,1)S(1)} %get-tuple-element.36.r_ref, bf16[640,5760]{1,0:T(8,128)(2,1)S(1)} %get-tuple-element.37.g_ref, ...), custom_call_target="tpu_custom_call", output_to_operand_aliasing={{0}: (4, {})} | custom-call | flops 10000000000 | tf_op jit(solution)/shard_map/pallas_call | solution.py:245
  58.1 1.5 %collective-permute-start.22 = (f32[63,8,128]{2,1,0:T(8,128)S(1)}, f32[63,8,128]{2,1,0:T(8,128)S(1)}, u32[]{:S(2)}, u32[]{:S(2)}) collective-permute-start(f32[63,8,128]{2,1,0:T(8,128)S(1)} %shard_map.107.refs_1_.refs_0_), channel_id=1, source_target_pairs={{0,2},{1,33},{2,0},{3,35},{4,6},{5,37},{6,4},{7,39},{8,10},{9,41},... | collective-permute-start | bytes 774152 | tf_op jit(solution)/shard_map/ppermute | solution.py:35
  59.6 2.1 %collective-permute-done.19.refs_1_ = f32[23,8,128]{2,1,0:T(8,128)S(1)} collective-permute-done((f32[23,8,128]{2,1,0:T(8,128)S(1)}, f32[23,8,128]{2,1,0:T(8,128)S(1)}, u32[]{:S(2)}, u32[]{:S(2)}) %collective-permute-start.19) | collective-permute-done | bytes 94240 | tf_op jit(solution)/shard_map/ppermute | solution.py:35
  61.7 3.0 %collective-permute-start.21 = (f32[23,8,128]{2,1,0:T(8,128)S(1)}, f32[23,8,128]{2,1,0:T(8,128)S(1)}, u32[]{:S(2)}, u32[]{:S(2)}) collective-permute-start(f32[23,8,128]{2,1,0:T(8,128)S(1)} %shard_map.109.rest_1_.refs_0_), channel_id=1, source_target_pairs={{0,96},{1,25},{2,98},{3,27},{4,100},{5,29},{6,102},{7,31},{8,104},... | collective-permute-start | bytes 282632 | tf_op jit(solution)/shard_map/ppermute | solution.py:35
  64.8 1.4 %shard_map.110 = (bf16[1,640,5760]{2,1,0:T(8,128)(2,1)}, f32[1,8,128]{2,1,0:T(8,128)S(1)}) custom-call(bf16[48,640]{1,0:T(8,128)(2,1)S(1)} %get-tuple-element.35.refs_2_.l_ref, bf16[48,5760]{1,0:T(8,128)(2,1)S(1)} %get-tuple-element.36.r_ref, bf16[640,5760]{1,0:T(8,128)(2,1)S(1)} %get-tuple-element.37.g_ref, ...), custom_call_target="tpu_custom_call", output_to_operand_aliasing={{0}: (4, {})} | custom-call | flops 10000000000 | tf_op jit(solution)/shard_map/pallas_call | solution.py:245
  66.3 5.3 %collective-permute-start.24 = (f32[125,8,128]{2,1,0:T(8,128)S(1)}, f32[125,8,128]{2,1,0:T(8,128)S(1)}, u32[]{:S(2)}, u32[]{:S(2)}) collective-permute-start(f32[125,8,128]{2,1,0:T(8,128)S(1)} %shard_map.111.refs_1_.refs_0_), channel_id=1, source_target_pairs={{0,1},{1,0},{2,3},{3,2},{4,5},{5,4},{6,7},{7,6},{8,9},{9,8},{10,11... | collective-permute-start | bytes 1536008 | tf_op jit(solution)/shard_map/ppermute | solution.py:39
  71.6 1.5 %collective-permute-start.23 = (f32[23,8,128]{2,1,0:T(8,128)S(1)}, f32[23,8,128]{2,1,0:T(8,128)S(1)}, u32[]{:S(2)}, u32[]{:S(2)}) collective-permute-start(f32[23,8,128]{2,1,0:T(8,128)S(1)} %shard_map.113.refs_2_.refs_0_), channel_id=1, source_target_pairs={{0,1},{1,0},{2,3},{3,2},{4,5},{5,4},{6,7},{7,6},{8,9},{9,8},{10,11... | collective-permute-start | bytes 282632 | tf_op jit(solution)/shard_map/ppermute | solution.py:39
  (69 shorter events, 13.2 us)
Async XLA Ops:
  0.6 9.7 %collective-permute-start.1 = (f32[200,1280]{1,0:T(8,128)}, f32[200,1280]{1,0:T(8,128)S(1)}, u32[]{:S(2)}, u32[]{:S(2)}) collective-permute-start(f32[200,1280]{1,0:T(8,128)} %refs_0_.1), channel_id=1, source_target_pairs={{0,1},{1,0},{2,3},{3,2},{4,5},{5,4},{6,7},{7,6},{8,9},{9,8},{10,11... | collective-permute-start | bytes 3072008 | tf_op jit(solution)/shard_map/ppermute | solution.py:39
  8.8 2.7 %collective-permute-start = (f32[5,8,128]{2,1,0:T(8,128)S(1)}, f32[5,8,128]{2,1,0:T(8,128)S(1)}, u32[]{:S(2)}, u32[]{:S(2)}) collective-permute-start(f32[5,8,128]{2,1,0:T(8,128)S(1)} %get-tuple-element.27.refs_2_.refs_0_), channel_id=1, source_target_pairs={{0,2},{1,33},{2,0},{3,35},{4,6},{5,37},{6,4},{7,39},{8,10},{9,41},... | collective-permute-start | bytes 61448 | tf_op jit(solution)/shard_map/ppermute | solution.py:35
  10.4 6.8 %collective-permute-start.4 = (f32[63,8,128]{2,1,0:T(8,128)S(1)}, f32[63,8,128]{2,1,0:T(8,128)S(1)}, u32[]{:S(2)}, u32[]{:S(2)}) collective-permute-start(f32[63,8,128]{2,1,0:T(8,128)S(1)} %get-tuple-element.28.refs_0_), channel_id=1, source_target_pairs={{0,2},{1,33},{2,0},{3,35},{4,6},{5,37},{6,4},{7,39},{8,10},{9,41},... | collective-permute-start | bytes 774152 | tf_op jit(solution)/shard_map/ppermute | solution.py:35
  11.6 4.0 %collective-permute-start.2 = (f32[5,8,128]{2,1,0:T(8,128)S(1)}, f32[5,8,128]{2,1,0:T(8,128)S(1)}, u32[]{:S(2)}, u32[]{:S(2)}) collective-permute-start(f32[5,8,128]{2,1,0:T(8,128)S(1)} %shard_map.78.refs_0_), channel_id=1, source_target_pairs={{0,6},{1,97},{2,4},{3,99},{4,2},{5,101},{6,0},{7,103},{8,14},{9,10... | collective-permute-start | bytes 61448 | tf_op jit(solution)/shard_map/ppermute | solution.py:35
  15.6 2.8 %collective-permute-start.3 = (f32[5,8,128]{2,1,0:T(8,128)S(1)}, f32[5,8,128]{2,1,0:T(8,128)S(1)}, u32[]{:S(2)}, u32[]{:S(2)}) collective-permute-start(f32[5,8,128]{2,1,0:T(8,128)S(1)} %shard_map.79.refs_2_.refs_0_), channel_id=1, source_target_pairs={{0,32},{1,9},{2,34},{3,11},{4,36},{5,13},{6,38},{7,15},{8,40},{9,1... | collective-permute-start | bytes 61448 | tf_op jit(solution)/shard_map/ppermute | solution.py:35
  17.2 4.7 %collective-permute-start.6 = (f32[32,8,128]{2,1,0:T(8,128)S(1)}, f32[32,8,128]{2,1,0:T(8,128)S(1)}, u32[]{:S(2)}, u32[]{:S(2)}) collective-permute-start(f32[32,8,128]{2,1,0:T(8,128)S(1)} %get-tuple-element.30.refs_0_), channel_id=1, source_target_pairs={{0,32},{1,9},{2,34},{3,11},{4,36},{5,13},{6,38},{7,15},{8,40},{9,1... | collective-permute-start | bytes 393224 | tf_op jit(solution)/shard_map/ppermute | solution.py:35
  18.4 5.4 %collective-permute-start.5 = (f32[5,8,128]{2,1,0:T(8,128)S(1)}, f32[5,8,128]{2,1,0:T(8,128)S(1)}, u32[]{:S(2)}, u32[]{:S(2)}) collective-permute-start(f32[5,8,128]{2,1,0:T(8,128)S(1)} %shard_map.82.refs_2_.refs_0_), channel_id=1, source_target_pairs={{0,96},{1,25},{2,98},{3,27},{4,100},{5,29},{6,102},{7,31},{8,104},... | collective-permute-start | bytes 61448 | tf_op jit(solution)/shard_map/ppermute | solution.py:35
  22.0 5.1 %collective-permute-start.8 = (f32[32,8,128]{2,1,0:T(8,128)S(1)}, f32[32,8,128]{2,1,0:T(8,128)S(1)}, u32[]{:S(2)}, u32[]{:S(2)}) collective-permute-start(f32[32,8,128]{2,1,0:T(8,128)S(1)} %shard_map.83.refs_0_), channel_id=1, source_target_pairs={{0,96},{1,25},{2,98},{3,27},{4,100},{5,29},{6,102},{7,31},{8,104},... | collective-permute-start | bytes 393224 | tf_op jit(solution)/shard_map/ppermute | solution.py:35
  23.8 3.9 %collective-permute-start.7 = (f32[5,8,128]{2,1,0:T(8,128)S(1)}, f32[5,8,128]{2,1,0:T(8,128)S(1)}, u32[]{:S(2)}, u32[]{:S(2)}) collective-permute-start(f32[5,8,128]{2,1,0:T(8,128)S(1)} %shard_map.85.refs_2_.refs_0_), channel_id=1, source_target_pairs={{0,24},{1,7},{2,26},{3,5},{4,28},{5,3},{6,30},{7,1},{8,16},{9,15},... | collective-permute-start | bytes 61448 | tf_op jit(solution)/shard_map/ppermute | solution.py:35
  27.7 2.8 %collective-permute-start.9 = (f32[5,8,128]{2,1,0:T(8,128)S(1)}, f32[5,8,128]{2,1,0:T(8,128)S(1)}, u32[]{:S(2)}, u32[]{:S(2)}) collective-permute-start(f32[5,8,128]{2,1,0:T(8,128)S(1)} %shard_map.88.refs_1_.refs_0_), channel_id=1, source_target_pairs={{0,8},{1,3},{2,10},{3,1},{4,12},{5,7},{6,14},{7,5},{8,0},{9,11},{1... | collective-permute-start | bytes 61448 | tf_op jit(solution)/shard_map/ppermute | solution.py:35
  30.5 6.9 %collective-permute-start.10 = (f32[5,8,128]{2,1,0:T(8,128)S(1)}, f32[5,8,128]{2,1,0:T(8,128)S(1)}, u32[]{:S(2)}, u32[]{:S(2)}) collective-permute-start(f32[5,8,128]{2,1,0:T(8,128)S(1)} %shard_map.91.refs_0_), channel_id=1, source_target_pairs={{0,1},{1,0},{2,3},{3,2},{4,5},{5,4},{6,7},{7,6},{8,9},{9,8},{10,11... | collective-permute-start | bytes 61448 | tf_op jit(solution)/shard_map/ppermute | solution.py:39
  36.5 6.1 %collective-permute-start.12 = (f32[32,8,128]{2,1,0:T(8,128)S(1)}, f32[32,8,128]{2,1,0:T(8,128)S(1)}, u32[]{:S(2)}, u32[]{:S(2)}) collective-permute-start(f32[32,8,128]{2,1,0:T(8,128)S(1)} %shard_map.89.refs_0_), channel_id=1, source_target_pairs={{0,8},{1,3},{2,10},{3,1},{4,12},{5,7},{6,14},{7,5},{8,0},{9,11},{1... | collective-permute-start | bytes 393224 | tf_op jit(solution)/shard_map/ppermute | solution.py:35
  40.1 5.0 %collective-permute-start.13 = (f32[23,8,128]{2,1,0:T(8,128)S(1)}, f32[23,8,128]{2,1,0:T(8,128)S(1)}, u32[]{:S(2)}, u32[]{:S(2)}) collective-permute-start(f32[23,8,128]{2,1,0:T(8,128)S(1)} %shard_map.95.refs_2_.rest_0_.refs_0_), channel_id=1, source_target_pairs={{0,6},{1,97},{2,4},{3,99},{4,2},{5,101},{6,0},{7,103},{8,14},{9,10... | collective-permute-start | bytes 282632 | tf_op jit(solution)/shard_map/ppermute | solution.py:35
  42.7 5.4 %collective-permute-start.15 = (f32[32,8,128]{2,1,0:T(8,128)S(1)}, f32[32,8,128]{2,1,0:T(8,128)S(1)}, u32[]{:S(2)}, u32[]{:S(2)}) collective-permute-start(f32[32,8,128]{2,1,0:T(8,128)S(1)} %shard_map.96.rest_1_.refs_0_), channel_id=1, source_target_pairs={{0,6},{1,97},{2,4},{3,99},{4,2},{5,101},{6,0},{7,103},{8,14},{9,10... | collective-permute-start | bytes 393224 | tf_op jit(solution)/shard_map/ppermute | solution.py:35
  45.1 5.2 %collective-permute-start.14 = (f32[23,8,128]{2,1,0:T(8,128)S(1)}, f32[23,8,128]{2,1,0:T(8,128)S(1)}, u32[]{:S(2)}, u32[]{:S(2)}) collective-permute-start(f32[23,8,128]{2,1,0:T(8,128)S(1)} %shard_map.98.refs_2_.refs_0_), channel_id=1, source_target_pairs={{0,24},{1,7},{2,26},{3,5},{4,28},{5,3},{6,30},{7,1},{8,16},{9,15},... | collective-permute-start | bytes 282632 | tf_op jit(solution)/shard_map/ppermute | solution.py:35
  48.1 5.1 %collective-permute-start.17 = (f32[32,8,128]{2,1,0:T(8,128)S(1)}, f32[32,8,128]{2,1,0:T(8,128)S(1)}, u32[]{:S(2)}, u32[]{:S(2)}) collective-permute-start(f32[32,8,128]{2,1,0:T(8,128)S(1)} %shard_map.99.refs_1_.refs_0_), channel_id=1, source_target_pairs={{0,24},{1,7},{2,26},{3,5},{4,28},{5,3},{6,30},{7,1},{8,16},{9,15},... | collective-permute-start | bytes 393224 | tf_op jit(solution)/shard_map/ppermute | solution.py:35
  50.4 3.8 %collective-permute-start.16 = (f32[23,8,128]{2,1,0:T(8,128)S(1)}, f32[23,8,128]{2,1,0:T(8,128)S(1)}, u32[]{:S(2)}, u32[]{:S(2)}) collective-permute-start(f32[23,8,128]{2,1,0:T(8,128)S(1)} %shard_map.101.refs_2_.refs_0_), channel_id=1, source_target_pairs={{0,32},{1,9},{2,34},{3,11},{4,36},{5,13},{6,38},{7,15},{8,40},{9,1... | collective-permute-start | bytes 282632 | tf_op jit(solution)/shard_map/ppermute | solution.py:35
  53.3 4.8 %collective-permute-start.20 = (f32[32,8,128]{2,1,0:T(8,128)S(1)}, f32[32,8,128]{2,1,0:T(8,128)S(1)}, u32[]{:S(2)}, u32[]{:S(2)}) collective-permute-start(f32[32,8,128]{2,1,0:T(8,128)S(1)} %shard_map.102.refs_1_.rest_2_.refs_0_), channel_id=1, source_target_pairs={{0,32},{1,9},{2,34},{3,11},{4,36},{5,13},{6,38},{7,15},{8,40},{9,1... | collective-permute-start | bytes 393224 | tf_op jit(solution)/shard_map/ppermute | solution.py:35
  54.2 3.7 %collective-permute-start.18 = (f32[23,8,128]{2,1,0:T(8,128)S(1)}, f32[23,8,128]{2,1,0:T(8,128)S(1)}, u32[]{:S(2)}, u32[]{:S(2)}) collective-permute-start(f32[23,8,128]{2,1,0:T(8,128)S(1)} %shard_map.104.rest_1_.refs_0_), channel_id=1, source_target_pairs={{0,8},{1,3},{2,10},{3,1},{4,12},{5,7},{6,14},{7,5},{8,0},{9,11},{1... | collective-permute-start | bytes 282632 | tf_op jit(solution)/shard_map/ppermute | solution.py:35
  57.9 3.8 %collective-permute-start.19 = (f32[23,8,128]{2,1,0:T(8,128)S(1)}, f32[23,8,128]{2,1,0:T(8,128)S(1)}, u32[]{:S(2)}, u32[]{:S(2)}) collective-permute-start(f32[23,8,128]{2,1,0:T(8,128)S(1)} %shard_map.106.refs_2_.refs_0_), channel_id=1, source_target_pairs={{0,2},{1,33},{2,0},{3,35},{4,6},{5,37},{6,4},{7,39},{8,10},{9,41},... | collective-permute-start | bytes 282632 | tf_op jit(solution)/shard_map/ppermute | solution.py:35
  58.1 8.1 %collective-permute-start.22 = (f32[63,8,128]{2,1,0:T(8,128)S(1)}, f32[63,8,128]{2,1,0:T(8,128)S(1)}, u32[]{:S(2)}, u32[]{:S(2)}) collective-permute-start(f32[63,8,128]{2,1,0:T(8,128)S(1)} %shard_map.107.refs_1_.refs_0_), channel_id=1, source_target_pairs={{0,2},{1,33},{2,0},{3,35},{4,6},{5,37},{6,4},{7,39},{8,10},{9,41},... | collective-permute-start | bytes 774152 | tf_op jit(solution)/shard_map/ppermute | solution.py:35
  61.7 9.8 %collective-permute-start.21 = (f32[23,8,128]{2,1,0:T(8,128)S(1)}, f32[23,8,128]{2,1,0:T(8,128)S(1)}, u32[]{:S(2)}, u32[]{:S(2)}) collective-permute-start(f32[23,8,128]{2,1,0:T(8,128)S(1)} %shard_map.109.rest_1_.refs_0_), channel_id=1, source_target_pairs={{0,96},{1,25},{2,98},{3,27},{4,100},{5,29},{6,102},{7,31},{8,104},... | collective-permute-start | bytes 282632 | tf_op jit(solution)/shard_map/ppermute | solution.py:35
  66.3 6.8 %collective-permute-start.24 = (f32[125,8,128]{2,1,0:T(8,128)S(1)}, f32[125,8,128]{2,1,0:T(8,128)S(1)}, u32[]{:S(2)}, u32[]{:S(2)}) collective-permute-start(f32[125,8,128]{2,1,0:T(8,128)S(1)} %shard_map.111.refs_1_.refs_0_), channel_id=1, source_target_pairs={{0,1},{1,0},{2,3},{3,2},{4,5},{5,4},{6,7},{7,6},{8,9},{9,8},{10,11... | collective-permute-start | bytes 1536008 | tf_op jit(solution)/shard_map/ppermute | solution.py:39
  71.6 2.5 %collective-permute-start.23 = (f32[23,8,128]{2,1,0:T(8,128)S(1)}, f32[23,8,128]{2,1,0:T(8,128)S(1)}, u32[]{:S(2)}, u32[]{:S(2)}) collective-permute-start(f32[23,8,128]{2,1,0:T(8,128)S(1)} %shard_map.113.refs_2_.refs_0_), channel_id=1, source_target_pairs={{0,1},{1,0},{2,3},{3,2},{4,5},{5,4},{6,7},{7,6},{8,9},{9,8},{10,11... | collective-permute-start | bytes 282632 | tf_op jit(solution)/shard_map/ppermute | solution.py:39
  (2 other events, 9.5 us)

commit v4 on v3

--- a/solution.py
+++ b/solution.py
@@ -13,7 +13,7 @@
 BF16 = jnp.bfloat16
 RING_BIT = {"x": 1, "z": 3, "y": 5}
 AROUND = ("x", "y", "z")
-P_HOPS = (("x0", "x1", "y0", "y1", "z1", "z0"), ("y0", "y1", "z0", "z1", "x1", "x0"))
+P_HOPS = (("x0", "x1", "y0", "y1", "z2", "z0"), ("y0", "y1", "z0", "z1", "x1", "x0"))
 Q_HOPS = (("x1", "z1", "y0", "z0", "x0", "y1"), ("y1", "x1", "z0", "x0", "y0", "z1"))
 HALVINGS = (0, 2)
 SLABS = (1, 0, 0, 3, 0, 1)
@@ -27,7 +27,7 @@
     bit = RING_BIT[ring]
     if level == "0":
         return index ^ (1 << bit)
-    return index ^ ((3 if ring in AROUND else 2) << bit)
+    return index ^ ((3 if level == "1" and ring in AROUND else 2) << bit)
 
 
 def swap(x, hops, step):
@@ -146,11 +146,12 @@
         )
         sub = lax.broadcasted_iota(jnp.int32, (rank, 1), 0)
         for j in range(rank):
-            scale = lax.rsqrt(gram[j : j + 1, j : j + 1])
-            column = jnp.where(sub > j, gram[:, j : j + 1] * scale, 0.0)
-            gram_row, total_row = gram[j : j + 1, :] * scale, total[j : j + 1, :] * scale
+            below = jnp.broadcast_to(jnp.where(sub > j, gram[:, j : j + 1], 0.0), gram.shape)
+            scale = lax.rsqrt(jnp.broadcast_to(gram[j : j + 1, j : j + 1], gram.shape))
+            gram_row, total_row = gram[j : j + 1, :] * scale[:1, :], total[j : j + 1, :] * scale[:1, :1]
+            column = below * scale
             gram = jnp.where(sub == j, gram_row, gram - column * gram_row)
-            total = jnp.where(sub == j, total_row, total - column * total_row)
+            total = jnp.where(sub == j, total_row, total - column[:, :1] * total_row)
         orth_ref[...] = total
         first = jnp.where(place() & 1 == 0, out_tiles - count, 0)
         product_tiles(total.astype(BF16), c_ref, first, send_ref)

time: 75.2 us -> 75.7 us (level)
  transfers between devices with their start and end apart: 25 -> 25, of which waited for: 14 -> 12; matrix products, arithmetic and copies ran while one was open for 0% -> 0% of each run, Pallas kernels for 21% -> 21%
where the time goes in v4:
time: 75.7 us; the launch traced here: 75.6 us
  starting transfers between devices  44.5 us (59%)
  Pallas kernels  17.1 us (23%)
  waiting for transfers between devices  13.1 us (17%)
  between operations  0.81 us (1%)
    ppermute x20, starting transfers between devices, swap(): lax.ppermute(x, AXES, [(i, partner(i, pair)) for i in range(lax.axis_size...  29.6 us
    ppermute x5, starting transfers between devices, swap_cores(): lax.ppermute(x, AXES, [(i, i ^ 1) for i in range(lax.axis_size(AXES))])  15 us
    ppermute x20, waiting for transfers between devices, swap(): lax.ppermute(x, AXES, [(i, partner(i, pair)) for i in range(lax.axis_size...  12.2 us
    pallas_call x1, Pallas kernels, left_product(): pl.pallas_call(body, in_specs=[pl.BlockSpec(memory_space=pltpu.HBM)] * 3,...  6.7 us
    pallas_call x3, Pallas kernels, residual_rows(): pl.pallas_call(body, in_specs=[vmem] * 4 + [anywhere] * len(others), out_...  5.48 us
    pallas_call x37, Pallas kernels, call(): pl.pallas_call(kernel, in_specs=[pl.BlockSpec(memory_space=pltpu.VMEM)] *...  4.94 us
  transfers between devices with their start and end apart: 25, of which 12 were waited for; matrix products, arithmetic and copies ran while one was open for 0% of the time, Pallas kernels for 21%

profile of v4, /device:TPU:1, one launch (start us, length us, event | category | flops | bytes accessed | tf_op | source)
XLA Modules:
  0.0 75.6 jit_solution(15890379610499514440)
XLA Ops:
  0.6 1.5 %collective-permute-start.1 = (f32[200,1280]{1,0:T(8,128)}, f32[200,1280]{1,0:T(8,128)S(1)}, u32[]{:S(2)}, u32[]{:S(2)}) collective-permute-start(f32[200,1280]{1,0:T(8,128)} %refs_0_.1), channel_id=1, source_target_pairs={{0,1},{1,0},{2,3},{3,2},{4,5},{5,4},{6,7},{7,6},{8,9},{9,8},{10,11... | collective-permute-start | bytes 3072008 | tf_op jit(solution)/shard_map/ppermute | solution.py:39
  2.1 6.7 %shard_map.75 = (f32[5,8,128]{2,1,0:T(8,128)S(1)}, bf16[640,5760]{1,0:T(8,128)(2,1)S(1)}, bf16[640,5760]{1,0:T(8,128)(2,1)S(1)}, bf16[640,5760]{1,0:T(8,128)(2,1)S(1)}) custom-call(bf16[1,640,5760]{2,1,0:T(8,128)(2,1)} %g_hbm.1, bf16[1,640,5760]{2,1,0:T(8,128)(2,1)} %r_hbm.1, f32[8,5760]{1,0:T(8,128)} %bitcast.2), custom_call_target="tpu_custom_call" | custom-call | tf_op jit(solution)/shard_map/pallas_call | solution.py:116
  8.8 1.5 %collective-permute-start = (f32[5,8,128]{2,1,0:T(8,128)S(1)}, f32[5,8,128]{2,1,0:T(8,128)S(1)}, u32[]{:S(2)}, u32[]{:S(2)}) collective-permute-start(f32[5,8,128]{2,1,0:T(8,128)S(1)} %get-tuple-element.27.refs_2_.refs_0_), channel_id=1, source_target_pairs={{0,2},{1,33},{2,0},{3,35},{4,6},{5,37},{6,4},{7,39},{8,10},{9,41},... | collective-permute-start | bytes 61448 | tf_op jit(solution)/shard_map/ppermute | solution.py:35
  11.6 2.8 %collective-permute-start.2 = (f32[5,8,128]{2,1,0:T(8,128)S(1)}, f32[5,8,128]{2,1,0:T(8,128)S(1)}, u32[]{:S(2)}, u32[]{:S(2)}) collective-permute-start(f32[5,8,128]{2,1,0:T(8,128)S(1)} %shard_map.78.refs_0_), channel_id=1, source_target_pairs={{0,6},{1,97},{2,4},{3,99},{4,2},{5,101},{6,0},{7,103},{8,14},{9,10... | collective-permute-start | bytes 61448 | tf_op jit(solution)/shard_map/ppermute | solution.py:35
  14.4 1.2 %collective-permute-done.2.refs_1_ = f32[5,8,128]{2,1,0:T(8,128)S(1)} collective-permute-done((f32[5,8,128]{2,1,0:T(8,128)S(1)}, f32[5,8,128]{2,1,0:T(8,128)S(1)}, u32[]{:S(2)}, u32[]{:S(2)}) %collective-permute-start.2) | collective-permute-done | bytes 20512 | tf_op jit(solution)/shard_map/ppermute | solution.py:35
  15.6 1.6 %collective-permute-start.3 = (f32[5,8,128]{2,1,0:T(8,128)S(1)}, f32[5,8,128]{2,1,0:T(8,128)S(1)}, u32[]{:S(2)}, u32[]{:S(2)}) collective-permute-start(f32[5,8,128]{2,1,0:T(8,128)S(1)} %shard_map.79.refs_2_.refs_0_), channel_id=1, source_target_pairs={{0,32},{1,9},{2,34},{3,11},{4,36},{5,13},{6,38},{7,15},{8,40},{9,1... | collective-permute-start | bytes 61448 | tf_op jit(solution)/shard_map/ppermute | solution.py:35
  18.4 3.6 %collective-permute-start.5 = (f32[5,8,128]{2,1,0:T(8,128)S(1)}, f32[5,8,128]{2,1,0:T(8,128)S(1)}, u32[]{:S(2)}, u32[]{:S(2)}) collective-permute-start(f32[5,8,128]{2,1,0:T(8,128)S(1)} %shard_map.82.refs_2_.refs_0_), channel_id=1, source_target_pairs={{0,96},{1,25},{2,98},{3,27},{4,100},{5,29},{6,102},{7,31},{8,104},... | collective-permute-start | bytes 61448 | tf_op jit(solution)/shard_map/ppermute | solution.py:35
  22.0 1.8 %collective-permute-start.8 = (f32[32,8,128]{2,1,0:T(8,128)S(1)}, f32[32,8,128]{2,1,0:T(8,128)S(1)}, u32[]{:S(2)}, u32[]{:S(2)}) collective-permute-start(f32[32,8,128]{2,1,0:T(8,128)S(1)} %shard_map.83.refs_0_), channel_id=1, source_target_pairs={{0,96},{1,25},{2,98},{3,27},{4,100},{5,29},{6,102},{7,31},{8,104},... | collective-permute-start | bytes 393224 | tf_op jit(solution)/shard_map/ppermute | solution.py:35
  23.8 2.6 %collective-permute-start.7 = (f32[5,8,128]{2,1,0:T(8,128)S(1)}, f32[5,8,128]{2,1,0:T(8,128)S(1)}, u32[]{:S(2)}, u32[]{:S(2)}) collective-permute-start(f32[5,8,128]{2,1,0:T(8,128)S(1)} %shard_map.85.refs_2_.refs_0_), channel_id=1, source_target_pairs={{0,16},{1,7},{2,18},{3,5},{4,20},{5,3},{6,22},{7,1},{8,24},{9,15},... | collective-permute-start | bytes 61448 | tf_op jit(solution)/shard_map/ppermute | solution.py:35
  28.5 2.1 %collective-permute-done.9.refs_1_ = f32[5,8,128]{2,1,0:T(8,128)S(1)} collective-permute-done((f32[5,8,128]{2,1,0:T(8,128)S(1)}, f32[5,8,128]{2,1,0:T(8,128)S(1)}, u32[]{:S(2)}, u32[]{:S(2)}) %collective-permute-start.9) | collective-permute-done | bytes 20512 | tf_op jit(solution)/shard_map/ppermute | solution.py:35
  30.5 5.9 %collective-permute-start.10 = (f32[5,8,128]{2,1,0:T(8,128)S(1)}, f32[5,8,128]{2,1,0:T(8,128)S(1)}, u32[]{:S(2)}, u32[]{:S(2)}) collective-permute-start(f32[5,8,128]{2,1,0:T(8,128)S(1)} %shard_map.91.refs_0_), channel_id=1, source_target_pairs={{0,1},{1,0},{2,3},{3,2},{4,5},{5,4},{6,7},{7,6},{8,9},{9,8},{10,11... | collective-permute-start | bytes 61448 | tf_op jit(solution)/shard_map/ppermute | solution.py:39
  37.2 1.6 %shard_map.92 = (f32[8,640]{1,0:T(8,128)S(1)}, f32[23,8,128]{2,1,0:T(8,128)S(1)}) custom-call(f32[5,8,128]{2,1,0:T(8,128)S(1)} %shard_map.91.refs_0_, f32[5,8,128]{2,1,0:T(8,128)S(1)} %collective-permute-done.10.refs_1_, bf16[640,5760]{1,0:T(8,128)(2,1)S(1)} %get-tuple-element.32.refs_2_.refs_1_), custom_call_target="tpu_custom_call" | custom-call | tf_op jit(solution)/shard_map/pallas_call | solution.py:73
  40.7 2.6 %collective-permute-start.13 = (f32[23,8,128]{2,1,0:T(8,128)S(1)}, f32[23,8,128]{2,1,0:T(8,128)S(1)}, u32[]{:S(2)}, u32[]{:S(2)}) collective-permute-start(f32[23,8,128]{2,1,0:T(8,128)S(1)} %shard_map.95.refs_2_.rest_0_.refs_0_), channel_id=1, source_target_pairs={{0,6},{1,97},{2,4},{3,99},{4,2},{5,101},{6,0},{7,103},{8,14},{9,10... | collective-permute-start | bytes 282632 | tf_op jit(solution)/shard_map/ppermute | solution.py:35
  43.5 1.4 %shard_map.97 = (bf16[1,640,5760]{2,1,0:T(8,128)(2,1)}, f32[1,8,128]{2,1,0:T(8,128)S(1)}) custom-call(bf16[48,640]{1,0:T(8,128)(2,1)S(1)} %get-tuple-element.35.refs_2_.l_ref, bf16[48,5760]{1,0:T(8,128)(2,1)S(1)} %get-tuple-element.36.r_ref, bf16[640,5760]{1,0:T(8,128)(2,1)S(1)} %get-tuple-element.37.g_ref, bf16[640,5760]{1,0:T(8,128)(2,1)S(1)} %get-tuple-element.38.e_ref, ...), custom_call_target="tpu_custom_call" | custom-call | flops 10000000000 | tf_op jit(solution)/shard_map/pallas_call | solution.py:246
  45.7 2.6 %collective-permute-start.14 = (f32[23,8,128]{2,1,0:T(8,128)S(1)}, f32[23,8,128]{2,1,0:T(8,128)S(1)}, u32[]{:S(2)}, u32[]{:S(2)}) collective-permute-start(f32[23,8,128]{2,1,0:T(8,128)S(1)} %shard_map.98.refs_2_.refs_0_), channel_id=1, source_target_pairs={{0,24},{1,7},{2,26},{3,5},{4,28},{5,3},{6,30},{7,1},{8,16},{9,15},... | collective-permute-start | bytes 282632 | tf_op jit(solution)/shard_map/ppermute | solution.py:35
  48.7 2.3 %collective-permute-start.17 = (f32[32,8,128]{2,1,0:T(8,128)S(1)}, f32[32,8,128]{2,1,0:T(8,128)S(1)}, u32[]{:S(2)}, u32[]{:S(2)}) collective-permute-start(f32[32,8,128]{2,1,0:T(8,128)S(1)} %shard_map.99.refs_1_.refs_0_), channel_id=1, source_target_pairs={{0,24},{1,7},{2,26},{3,5},{4,28},{5,3},{6,30},{7,1},{8,16},{9,15},... | collective-permute-start | bytes 393224 | tf_op jit(solution)/shard_map/ppermute | solution.py:35
  51.9 1.9 %collective-permute-done.17.refs_1_ = f32[32,8,128]{2,1,0:T(8,128)S(1)} collective-permute-done((f32[32,8,128]{2,1,0:T(8,128)S(1)}, f32[32,8,128]{2,1,0:T(8,128)S(1)}, u32[]{:S(2)}, u32[]{:S(2)}) %collective-permute-start.17) | collective-permute-done | bytes 131104 | tf_op jit(solution)/shard_map/ppermute | solution.py:35
  55.0 2.6 %shard_map.105 = (bf16[1,640,5760]{2,1,0:T(8,128)(2,1)}, f32[1,8,128]{2,1,0:T(8,128)S(1)}) custom-call(bf16[48,640]{1,0:T(8,128)(2,1)S(1)} %get-tuple-element.35.refs_2_.l_ref, bf16[48,5760]{1,0:T(8,128)(2,1)S(1)} %get-tuple-element.36.r_ref, bf16[640,5760]{1,0:T(8,128)(2,1)S(1)} %get-tuple-element.37.g_ref, ...), custom_call_target="tpu_custom_call", output_to_operand_aliasing={{0}: (4, {})} | custom-call | flops 10000000000 | tf_op jit(solution)/shard_map/pallas_call | solution.py:246
  58.6 1.5 %collective-permute-start.22 = (f32[63,8,128]{2,1,0:T(8,128)S(1)}, f32[63,8,128]{2,1,0:T(8,128)S(1)}, u32[]{:S(2)}, u32[]{:S(2)}) collective-permute-start(f32[63,8,128]{2,1,0:T(8,128)S(1)} %shard_map.107.refs_1_.refs_0_), channel_id=1, source_target_pairs={{0,2},{1,33},{2,0},{3,35},{4,6},{5,37},{6,4},{7,39},{8,10},{9,41},... | collective-permute-start | bytes 774152 | tf_op jit(solution)/shard_map/ppermute | solution.py:35
  60.1 2.1 %collective-permute-done.19.refs_1_ = f32[23,8,128]{2,1,0:T(8,128)S(1)} collective-permute-done((f32[23,8,128]{2,1,0:T(8,128)S(1)}, f32[23,8,128]{2,1,0:T(8,128)S(1)}, u32[]{:S(2)}, u32[]{:S(2)}) %collective-permute-start.19) | collective-permute-done | bytes 94240 | tf_op jit(solution)/shard_map/ppermute | solution.py:35
  62.3 3.0 %collective-permute-start.21 = (f32[23,8,128]{2,1,0:T(8,128)S(1)}, f32[23,8,128]{2,1,0:T(8,128)S(1)}, u32[]{:S(2)}, u32[]{:S(2)}) collective-permute-start(f32[23,8,128]{2,1,0:T(8,128)S(1)} %shard_map.109.rest_1_.refs_0_), channel_id=1, source_target_pairs={{0,96},{1,25},{2,98},{3,27},{4,100},{5,29},{6,102},{7,31},{8,104},... | collective-permute-start | bytes 282632 | tf_op jit(solution)/shard_map/ppermute | solution.py:35
  65.3 1.4 %shard_map.110 = (bf16[1,640,5760]{2,1,0:T(8,128)(2,1)}, f32[1,8,128]{2,1,0:T(8,128)S(1)}) custom-call(bf16[48,640]{1,0:T(8,128)(2,1)S(1)} %get-tuple-element.35.refs_2_.l_ref, bf16[48,5760]{1,0:T(8,128)(2,1)S(1)} %get-tuple-element.36.r_ref, bf16[640,5760]{1,0:T(8,128)(2,1)S(1)} %get-tuple-element.37.g_ref, ...), custom_call_target="tpu_custom_call", output_to_operand_aliasing={{0}: (4, {})} | custom-call | flops 10000000000 | tf_op jit(solution)/shard_map/pallas_call | solution.py:246
  66.8 5.3 %collective-permute-start.24 = (f32[125,8,128]{2,1,0:T(8,128)S(1)}, f32[125,8,128]{2,1,0:T(8,128)S(1)}, u32[]{:S(2)}, u32[]{:S(2)}) collective-permute-start(f32[125,8,128]{2,1,0:T(8,128)S(1)} %shard_map.111.refs_1_.refs_0_), channel_id=1, source_target_pairs={{0,1},{1,0},{2,3},{3,2},{4,5},{5,4},{6,7},{7,6},{8,9},{9,8},{10,11... | collective-permute-start | bytes 1536008 | tf_op jit(solution)/shard_map/ppermute | solution.py:39
  72.1 1.5 %collective-permute-start.23 = (f32[23,8,128]{2,1,0:T(8,128)S(1)}, f32[23,8,128]{2,1,0:T(8,128)S(1)}, u32[]{:S(2)}, u32[]{:S(2)}) collective-permute-start(f32[23,8,128]{2,1,0:T(8,128)S(1)} %shard_map.113.refs_2_.refs_0_), channel_id=1, source_target_pairs={{0,1},{1,0},{2,3},{3,2},{4,5},{5,4},{6,7},{7,6},{8,9},{9,8},{10,11... | collective-permute-start | bytes 282632 | tf_op jit(solution)/shard_map/ppermute | solution.py:39
  (69 shorter events, 13.8 us)
Async XLA Ops:
  0.6 9.7 %collective-permute-start.1 = (f32[200,1280]{1,0:T(8,128)}, f32[200,1280]{1,0:T(8,128)S(1)}, u32[]{:S(2)}, u32[]{:S(2)}) collective-permute-start(f32[200,1280]{1,0:T(8,128)} %refs_0_.1), channel_id=1, source_target_pairs={{0,1},{1,0},{2,3},{3,2},{4,5},{5,4},{6,7},{7,6},{8,9},{9,8},{10,11... | collective-permute-start | bytes 3072008 | tf_op jit(solution)/shard_map/ppermute | solution.py:39
  8.8 2.7 %collective-permute-start = (f32[5,8,128]{2,1,0:T(8,128)S(1)}, f32[5,8,128]{2,1,0:T(8,128)S(1)}, u32[]{:S(2)}, u32[]{:S(2)}) collective-permute-start(f32[5,8,128]{2,1,0:T(8,128)S(1)} %get-tuple-element.27.refs_2_.refs_0_), channel_id=1, source_target_pairs={{0,2},{1,33},{2,0},{3,35},{4,6},{5,37},{6,4},{7,39},{8,10},{9,41},... | collective-permute-start | bytes 61448 | tf_op jit(solution)/shard_map/ppermute | solution.py:35
  10.4 6.8 %collective-permute-start.4 = (f32[63,8,128]{2,1,0:T(8,128)S(1)}, f32[63,8,128]{2,1,0:T(8,128)S(1)}, u32[]{:S(2)}, u32[]{:S(2)}) collective-permute-start(f32[63,8,128]{2,1,0:T(8,128)S(1)} %get-tuple-element.28.refs_0_), channel_id=1, source_target_pairs={{0,2},{1,33},{2,0},{3,35},{4,6},{5,37},{6,4},{7,39},{8,10},{9,41},... | collective-permute-start | bytes 774152 | tf_op jit(solution)/shard_map/ppermute | solution.py:35
  11.6 4.0 %collective-permute-start.2 = (f32[5,8,128]{2,1,0:T(8,128)S(1)}, f32[5,8,128]{2,1,0:T(8,128)S(1)}, u32[]{:S(2)}, u32[]{:S(2)}) collective-permute-start(f32[5,8,128]{2,1,0:T(8,128)S(1)} %shard_map.78.refs_0_), channel_id=1, source_target_pairs={{0,6},{1,97},{2,4},{3,99},{4,2},{5,101},{6,0},{7,103},{8,14},{9,10... | collective-permute-start | bytes 61448 | tf_op jit(solution)/shard_map/ppermute | solution.py:35
  15.6 2.8 %collective-permute-start.3 = (f32[5,8,128]{2,1,0:T(8,128)S(1)}, f32[5,8,128]{2,1,0:T(8,128)S(1)}, u32[]{:S(2)}, u32[]{:S(2)}) collective-permute-start(f32[5,8,128]{2,1,0:T(8,128)S(1)} %shard_map.79.refs_2_.refs_0_), channel_id=1, source_target_pairs={{0,32},{1,9},{2,34},{3,11},{4,36},{5,13},{6,38},{7,15},{8,40},{9,1... | collective-permute-start | bytes 61448 | tf_op jit(solution)/shard_map/ppermute | solution.py:35
  17.2 4.7 %collective-permute-start.6 = (f32[32,8,128]{2,1,0:T(8,128)S(1)}, f32[32,8,128]{2,1,0:T(8,128)S(1)}, u32[]{:S(2)}, u32[]{:S(2)}) collective-permute-start(f32[32,8,128]{2,1,0:T(8,128)S(1)} %get-tuple-element.30.refs_0_), channel_id=1, source_target_pairs={{0,32},{1,9},{2,34},{3,11},{4,36},{5,13},{6,38},{7,15},{8,40},{9,1... | collective-permute-start | bytes 393224 | tf_op jit(solution)/shard_map/ppermute | solution.py:35
  18.4 5.4 %collective-permute-start.5 = (f32[5,8,128]{2,1,0:T(8,128)S(1)}, f32[5,8,128]{2,1,0:T(8,128)S(1)}, u32[]{:S(2)}, u32[]{:S(2)}) collective-permute-start(f32[5,8,128]{2,1,0:T(8,128)S(1)} %shard_map.82.refs_2_.refs_0_), channel_id=1, source_target_pairs={{0,96},{1,25},{2,98},{3,27},{4,100},{5,29},{6,102},{7,31},{8,104},... | collective-permute-start | bytes 61448 | tf_op jit(solution)/shard_map/ppermute | solution.py:35
  22.0 5.1 %collective-permute-start.8 = (f32[32,8,128]{2,1,0:T(8,128)S(1)}, f32[32,8,128]{2,1,0:T(8,128)S(1)}, u32[]{:S(2)}, u32[]{:S(2)}) collective-permute-start(f32[32,8,128]{2,1,0:T(8,128)S(1)} %shard_map.83.refs_0_), channel_id=1, source_target_pairs={{0,96},{1,25},{2,98},{3,27},{4,100},{5,29},{6,102},{7,31},{8,104},... | collective-permute-start | bytes 393224 | tf_op jit(solution)/shard_map/ppermute | solution.py:35
  23.8 3.9 %collective-permute-start.7 = (f32[5,8,128]{2,1,0:T(8,128)S(1)}, f32[5,8,128]{2,1,0:T(8,128)S(1)}, u32[]{:S(2)}, u32[]{:S(2)}) collective-permute-start(f32[5,8,128]{2,1,0:T(8,128)S(1)} %shard_map.85.refs_2_.refs_0_), channel_id=1, source_target_pairs={{0,16},{1,7},{2,18},{3,5},{4,20},{5,3},{6,22},{7,1},{8,24},{9,15},... | collective-permute-start | bytes 61448 | tf_op jit(solution)/shard_map/ppermute | solution.py:35
  27.7 2.8 %collective-permute-start.9 = (f32[5,8,128]{2,1,0:T(8,128)S(1)}, f32[5,8,128]{2,1,0:T(8,128)S(1)}, u32[]{:S(2)}, u32[]{:S(2)}) collective-permute-start(f32[5,8,128]{2,1,0:T(8,128)S(1)} %shard_map.88.refs_1_.refs_0_), channel_id=1, source_target_pairs={{0,8},{1,3},{2,10},{3,1},{4,12},{5,7},{6,14},{7,5},{8,0},{9,11},{1... | collective-permute-start | bytes 61448 | tf_op jit(solution)/shard_map/ppermute | solution.py:35
  30.5 6.7 %collective-permute-start.10 = (f32[5,8,128]{2,1,0:T(8,128)S(1)}, f32[5,8,128]{2,1,0:T(8,128)S(1)}, u32[]{:S(2)}, u32[]{:S(2)}) collective-permute-start(f32[5,8,128]{2,1,0:T(8,128)S(1)} %shard_map.91.refs_0_), channel_id=1, source_target_pairs={{0,1},{1,0},{2,3},{3,2},{4,5},{5,4},{6,7},{7,6},{8,9},{9,8},{10,11... | collective-permute-start | bytes 61448 | tf_op jit(solution)/shard_map/ppermute | solution.py:39
  36.4 6.8 %collective-permute-start.12 = (f32[32,8,128]{2,1,0:T(8,128)S(1)}, f32[32,8,128]{2,1,0:T(8,128)S(1)}, u32[]{:S(2)}, u32[]{:S(2)}) collective-permute-start(f32[32,8,128]{2,1,0:T(8,128)S(1)} %shard_map.89.refs_0_), channel_id=1, source_target_pairs={{0,8},{1,3},{2,10},{3,1},{4,12},{5,7},{6,14},{7,5},{8,0},{9,11},{1... | collective-permute-start | bytes 393224 | tf_op jit(solution)/shard_map/ppermute | solution.py:35
  40.7 5.0 %collective-permute-start.13 = (f32[23,8,128]{2,1,0:T(8,128)S(1)}, f32[23,8,128]{2,1,0:T(8,128)S(1)}, u32[]{:S(2)}, u32[]{:S(2)}) collective-permute-start(f32[23,8,128]{2,1,0:T(8,128)S(1)} %shard_map.95.refs_2_.rest_0_.refs_0_), channel_id=1, source_target_pairs={{0,6},{1,97},{2,4},{3,99},{4,2},{5,101},{6,0},{7,103},{8,14},{9,10... | collective-permute-start | bytes 282632 | tf_op jit(solution)/shard_map/ppermute | solution.py:35
  43.2 5.4 %collective-permute-start.15 = (f32[32,8,128]{2,1,0:T(8,128)S(1)}, f32[32,8,128]{2,1,0:T(8,128)S(1)}, u32[]{:S(2)}, u32[]{:S(2)}) collective-permute-start(f32[32,8,128]{2,1,0:T(8,128)S(1)} %shard_map.96.rest_1_.refs_0_), channel_id=1, source_target_pairs={{0,6},{1,97},{2,4},{3,99},{4,2},{5,101},{6,0},{7,103},{8,14},{9,10... | collective-permute-start | bytes 393224 | tf_op jit(solution)/shard_map/ppermute | solution.py:35
  45.7 5.2 %collective-permute-start.14 = (f32[23,8,128]{2,1,0:T(8,128)S(1)}, f32[23,8,128]{2,1,0:T(8,128)S(1)}, u32[]{:S(2)}, u32[]{:S(2)}) collective-permute-start(f32[23,8,128]{2,1,0:T(8,128)S(1)} %shard_map.98.refs_2_.refs_0_), channel_id=1, source_target_pairs={{0,24},{1,7},{2,26},{3,5},{4,28},{5,3},{6,30},{7,1},{8,16},{9,15},... | collective-permute-start | bytes 282632 | tf_op jit(solution)/shard_map/ppermute | solution.py:35
  48.7 5.1 %collective-permute-start.17 = (f32[32,8,128]{2,1,0:T(8,128)S(1)}, f32[32,8,128]{2,1,0:T(8,128)S(1)}, u32[]{:S(2)}, u32[]{:S(2)}) collective-permute-start(f32[32,8,128]{2,1,0:T(8,128)S(1)} %shard_map.99.refs_1_.refs_0_), channel_id=1, source_target_pairs={{0,24},{1,7},{2,26},{3,5},{4,28},{5,3},{6,30},{7,1},{8,16},{9,15},... | collective-permute-start | bytes 393224 | tf_op jit(solution)/shard_map/ppermute | solution.py:35
  50.9 3.8 %collective-permute-start.16 = (f32[23,8,128]{2,1,0:T(8,128)S(1)}, f32[23,8,128]{2,1,0:T(8,128)S(1)}, u32[]{:S(2)}, u32[]{:S(2)}) collective-permute-start(f32[23,8,128]{2,1,0:T(8,128)S(1)} %shard_map.101.refs_2_.refs_0_), channel_id=1, source_target_pairs={{0,32},{1,9},{2,34},{3,11},{4,36},{5,13},{6,38},{7,15},{8,40},{9,1... | collective-permute-start | bytes 282632 | tf_op jit(solution)/shard_map/ppermute | solution.py:35
  53.8 4.8 %collective-permute-start.20 = (f32[32,8,128]{2,1,0:T(8,128)S(1)}, f32[32,8,128]{2,1,0:T(8,128)S(1)}, u32[]{:S(2)}, u32[]{:S(2)}) collective-permute-start(f32[32,8,128]{2,1,0:T(8,128)S(1)} %shard_map.102.refs_1_.rest_2_.refs_0_), channel_id=1, source_target_pairs={{0,32},{1,9},{2,34},{3,11},{4,36},{5,13},{6,38},{7,15},{8,40},{9,1... | collective-permute-start | bytes 393224 | tf_op jit(solution)/shard_map/ppermute | solution.py:35
  54.8 3.7 %collective-permute-start.18 = (f32[23,8,128]{2,1,0:T(8,128)S(1)}, f32[23,8,128]{2,1,0:T(8,128)S(1)}, u32[]{:S(2)}, u32[]{:S(2)}) collective-permute-start(f32[23,8,128]{2,1,0:T(8,128)S(1)} %shard_map.104.rest_1_.refs_0_), channel_id=1, source_target_pairs={{0,8},{1,3},{2,10},{3,1},{4,12},{5,7},{6,14},{7,5},{8,0},{9,11},{1... | collective-permute-start | bytes 282632 | tf_op jit(solution)/shard_map/ppermute | solution.py:35
  58.5 3.8 %collective-permute-start.19 = (f32[23,8,128]{2,1,0:T(8,128)S(1)}, f32[23,8,128]{2,1,0:T(8,128)S(1)}, u32[]{:S(2)}, u32[]{:S(2)}) collective-permute-start(f32[23,8,128]{2,1,0:T(8,128)S(1)} %shard_map.106.refs_2_.refs_0_), channel_id=1, source_target_pairs={{0,2},{1,33},{2,0},{3,35},{4,6},{5,37},{6,4},{7,39},{8,10},{9,41},... | collective-permute-start | bytes 282632 | tf_op jit(solution)/shard_map/ppermute | solution.py:35
  58.6 8.1 %collective-permute-start.22 = (f32[63,8,128]{2,1,0:T(8,128)S(1)}, f32[63,8,128]{2,1,0:T(8,128)S(1)}, u32[]{:S(2)}, u32[]{:S(2)}) collective-permute-start(f32[63,8,128]{2,1,0:T(8,128)S(1)} %shard_map.107.refs_1_.refs_0_), channel_id=1, source_target_pairs={{0,2},{1,33},{2,0},{3,35},{4,6},{5,37},{6,4},{7,39},{8,10},{9,41},... | collective-permute-start | bytes 774152 | tf_op jit(solution)/shard_map/ppermute | solution.py:35
  62.3 9.8 %collective-permute-start.21 = (f32[23,8,128]{2,1,0:T(8,128)S(1)}, f32[23,8,128]{2,1,0:T(8,128)S(1)}, u32[]{:S(2)}, u32[]{:S(2)}) collective-permute-start(f32[23,8,128]{2,1,0:T(8,128)S(1)} %shard_map.109.rest_1_.refs_0_), channel_id=1, source_target_pairs={{0,96},{1,25},{2,98},{3,27},{4,100},{5,29},{6,102},{7,31},{8,104},... | collective-permute-start | bytes 282632 | tf_op jit(solution)/shard_map/ppermute | solution.py:35
  66.8 6.8 %collective-permute-start.24 = (f32[125,8,128]{2,1,0:T(8,128)S(1)}, f32[125,8,128]{2,1,0:T(8,128)S(1)}, u32[]{:S(2)}, u32[]{:S(2)}) collective-permute-start(f32[125,8,128]{2,1,0:T(8,128)S(1)} %shard_map.111.refs_1_.refs_0_), channel_id=1, source_target_pairs={{0,1},{1,0},{2,3},{3,2},{4,5},{5,4},{6,7},{7,6},{8,9},{9,8},{10,11... | collective-permute-start | bytes 1536008 | tf_op jit(solution)/shard_map/ppermute | solution.py:39
  72.1 2.5 %collective-permute-start.23 = (f32[23,8,128]{2,1,0:T(8,128)S(1)}, f32[23,8,128]{2,1,0:T(8,128)S(1)}, u32[]{:S(2)}, u32[]{:S(2)}) collective-permute-start(f32[23,8,128]{2,1,0:T(8,128)S(1)} %shard_map.113.refs_2_.refs_0_), channel_id=1, source_target_pairs={{0,1},{1,0},{2,3},{3,2},{4,5},{5,4},{6,7},{7,6},{8,9},{9,8},{10,11... | collective-permute-start | bytes 282632 | tf_op jit(solution)/shard_map/ppermute | solution.py:39
  (2 other events, 10.0 us)
